TPU v7x, 256 devices: a whole 4x4x8 slice. The times are simulated.
256 devices in a mesh: dp: 16 (over z, core), slab: 4 (over x), fsdp: 4 (over y).
Axes of the slice: x: 4, y: 4, z: 8, core: 2. Of those that a mesh axis runs over, the one named last changes fastest.
Arguments:
- pixels: bfloat16 [16, 4, 16, 3, 224, 224], P('dp', 'fsdp', 'slab'), may hold values from -6 to 6
- grad_norm: bfloat16 [4, 4, 8192, 1280], P('slab', 'fsdp', 'dp'), may hold values from -0.015625 to 0.015625
- grad_resid: bfloat16 [4, 4, 8192, 1280], P('slab', 'fsdp', 'dp'), may hold values from -0.015625 to 0.015625
- embed_weight: bfloat16 [1280, 1176], P('fsdp'), may hold values from -0.1875 to 0.1875
- norm_gain: float32 [1280], replicated, may hold values from 0.1 to 1.9
- send_slot: int32 [4, 4, 8192], P('slab', 'fsdp', 'dp'), may hold values from 0 to 1023, as said below
- recv_slot: int32 [4, 4, 8192], P('slab', 'fsdp', 'dp'), may hold values from 0 to 1023, as said below
Outputs:
- embed_grad: float32 [1280, 1176], P('fsdp')
- norm_grad: float32 [2, 1280], P(None, 'fsdp')
Inputs may be any that keep to these rules, and one draw needn't show every extreme that they name: `send_slot`: within each slab and fsdp index, the rows of the dp group are a one-to-one map onto the tokens of the group's slab owners: each device sends all its 512 rows and its tokens receive exactly 512; the ranks of the rows from one device to one device run from 0 up without gaps; at most 64 rows go from one device to one device, and that many do in every draw. `recv_slot`: the inverse of send_slot: the values of one device are distinct and name each row that is sent to it exactly once.
All inputs are finite; a program needn't handle non-finite values.
Results may differ from a plain program's by a relative error of at most 0.0029.
Values may be sent and summed in bfloat16 or wider, within the bound.
No kernel may reach another device: no remote copies, remote signals or barrier semaphores. Data moves between devices by JAX's collectives and lax.ppermute only.
A program may use at most 128 MiB of HBM per device.

v0:
```python
import jax
import jax.numpy as jnp
from jax import lax
from jax.sharding import PartitionSpec as P

GH = 16
GW = 16


def shifted(array, axis, by):
    length = lax.axis_size(axis)
    pairs = [(i, i + by) for i in range(length) if 0 <= i + by < length]
    return lax.ppermute(array, axis, pairs)


def to_rows(frame_pairs):
    temporal, _, colours, height, width = frame_pairs.shape
    patch_size = height // GH
    split = frame_pairs.reshape(temporal, 2, colours, GH, patch_size, GW, patch_size)
    ordered = jnp.transpose(split, (0, 3, 5, 2, 1, 4, 6))
    return ordered.reshape(temporal * GH * GW, 2 * colours * patch_size * patch_size)


def shards(pixels, grad_norm, grad_resid, embed_weight, norm_gain, send_slot, recv_slot):
    frames = pixels[0, 0]
    earlier = shifted(frames[-1], "slab", 1)
    before = jnp.concatenate([earlier[None], frames[1:-1:2]], axis=0)
    frame_pairs = jnp.stack([before, frames[0::2]], axis=1)
    patches = to_rows(frame_pairs)
    row_count = grad_norm.shape[2]
    model_width = grad_norm.shape[3]
    patch_width = patches.shape[1]
    groups = lax.axis_size("dp")
    capacity = 2 * row_count // groups
    send_index = send_slot[0, 0]
    take_index = recv_slot[0, 0]
    both = jnp.concatenate([grad_norm[0, 0], grad_resid[0, 0]], axis=1)
    packed = jnp.zeros((groups * capacity, 2 * model_width), jnp.bfloat16).at[send_index].set(both)
    arrived = lax.all_to_all(
        packed.reshape(groups, capacity, 2 * model_width),
        "dp",
        split_axis=0,
        concat_axis=0,
        tiled=True,
    )
    gradients = arrived.reshape(groups * capacity, 2 * model_width)[take_index]
    grad_rows = gradients[:, :model_width]
    resid_rows = gradients[:, model_width:]
    embedded = lax.dot_general(
        patches,
        lax.all_gather(embed_weight, "fsdp", axis=0, tiled=True),
        (((1,), (1,)), ((), ())),
        preferred_element_type=jnp.float32,
    )
    center = jnp.mean(embedded, axis=-1, keepdims=True)
    deviation = embedded - center
    variance = jnp.mean(deviation * deviation, axis=-1, keepdims=True)
    inverse_std = lax.rsqrt(variance + 1e-06)
    normalized = deviation * inverse_std
    upstream_norm = grad_rows.astype(jnp.float32)
    upstream = upstream_norm * norm_gain
    inner = jnp.mean(upstream * normalized, axis=-1, keepdims=True)
    input_grad = resid_rows.astype(jnp.float32) + inverse_std * (
        upstream - jnp.mean(upstream, axis=-1, keepdims=True) - normalized * inner
    )
    input_grad = input_grad.astype(jnp.bfloat16)
    gain_terms = upstream_norm * normalized
    product = lax.dot_general(
        input_grad, patches, (((0,), (0,)), ((), ())), preferred_element_type=jnp.float32
    )
    gain_sum = jnp.sum(gain_terms, axis=0)
    bias_sum = jnp.sum(upstream_norm, axis=0)
    scattered = lax.psum_scatter(
        jnp.concatenate([product, gain_sum[:, None], bias_sum[:, None]], axis=1),
        "fsdp",
        scatter_dimension=0,
        tiled=True,
    )
    summed = lax.psum(scattered, ("dp", "slab"))
    embed_grad = summed[:, :patch_width]
    norm_grad = jnp.transpose(summed[:, patch_width:])
    return (embed_grad, norm_grad)


def solution(mesh):
    return jax.shard_map(
        shards,
        mesh=mesh,
        in_specs=(
            P("dp", "fsdp", "slab", None, None, None),
            P("slab", "fsdp", "dp", None),
            P("slab", "fsdp", "dp", None),
            P("fsdp", None),
            P(),
            P("slab", "fsdp", "dp"),
            P("slab", "fsdp", "dp"),
        ),
        out_specs=(P("fsdp", None), P(None, "fsdp")),
        check_vma=False,
    )
```

profile of v0, /device:TPU:1, one launch (start us, length us, event | category | flops | bytes accessed | tf_op | source)
XLA Modules:
  0.0 452.5 jit_solution(10342576476237291866)
XLA Ops:
  7.8 8.6 %scatter_custom_fusion = bf16[1024,2560]{1,0:T(8,128)(2,1)} fusion(s32[512]{0:T(512)S(1)} %bitcast.36, bf16[512,1280]{1,0:T(8,128)(2,1)} %bitcast.33, bf16[]{:T(256)} %constant.21, bf16[512,1280]{1,0:T(8,128)(2,1)} %bitcast.34, bf16[]{:T(256)} %constant.4.clone.1), kind=kCustom, calls=%fused_computation.15 | custom fusion | flops 5242880 | bytes 7864324 | tf_op jit(solution)/shard_map/scatter | solution.py:38
  16.4 10.1 %all-to-all-start = ((bf16[16,64,2560]{2,1,0:T(8,128)(2,1)}), bf16[16,64,2560]{2,1,0:T(8,128)(2,1)}, u32[]{:S(2)}, u32[]{:S(2)}) async-start(bf16[16,64,2560]{2,1,0:T(8,128)(2,1)} %bitcast.31), calls=%async_computation | async-start | bytes 10485760 | tf_op jit(solution)/shard_map/all_to_all | solution.py:39
  27.3 0.8 slice_bitcast_fusion
  28.1 3.8 collective-permute-start
  32.0 3.3 concatenate.17
  35.3 1.1 slice.27
  36.5 7.8 %stack.7 = bf16[2,1,3,16,14,16,14]{6,5,4,3,2,0,1:T(8,128)(2,1)} reshape(bf16[2,3,224,224]{3,2,1,0:T(8,128)(2,1)S(1)} %slice.27) | data formatting | bytes 1204224 | tf_op jit(solution)/shard_map/stack | solution.py:28
  44.2 5.4 %concatenate.16 = bf16[1,1,3,16,14,16,14]{6,5,4,3,2,1,0:T(8,128)(2,1)} reshape(bf16[3,224,224]{2,1,0:T(8,128)(2,1)} %collective-permute-done) | data formatting | bytes 602112 | tf_op jit(solution)/shard_map/concatenate | solution.py:27
  49.7 9.6 %maximum_bitcast_fusion = bf16[2,16,16,3,2,14,14]{6,2,5,1,3,4,0:T(8,128)(2,1)} fusion(bf16[2,1,3,16,14,16,14]{6,5,4,3,2,1,0:T(8,128)(2,1)} %bitcast.30, bf16[1,1,3,16,14,16,14]{6,5,4,3,2,1,0:T(8,128)(2,1)S(1)} %concatenate.17, bf16[1,1,3,16,14,16,14]{6,5,4,3,2,1,0:T(8,128)(2,1)} %concatenate.16), kind=kLoop, calls=%fused_computation.2 | loop fusion | flops 1204224 | bytes 2408448 | tf_op jit(solution)/shard_map/transpose | solution.py:20
  59.3 24.5 %copy.15 = bf16[2,16,16,3,2,14,14]{2,1,0,6,5,4,3:T(8,128)(2,1)} copy(bf16[2,16,16,3,2,14,14]{6,2,5,1,3,4,0:T(8,128)(2,1)} %maximum_bitcast_fusion) | data formatting | bytes 2408448 | tf_op jit(solution)/shard_map/transpose | solution.py:20
  83.8 17.2 %reshape.104 = bf16[512,1176]{0,1:T(8,128)(2,1)} reshape(bf16[2,16,16,3,2,14,14]{2,1,0,6,5,4,3:T(8,128)(2,1)} %copy.15) | data formatting | bytes 2408448 | tf_op jit(solution)/shard_map/reshape | solution.py:21
  101.0 4.3 fusion.23
  105.8 36.8 %all-to-all-done = bf16[16,64,2560]{2,1,0:T(8,128)(2,1)} async-done(((bf16[16,64,2560]{2,1,0:T(8,128)(2,1)}), bf16[16,64,2560]{2,1,0:T(8,128)(2,1)}, u32[]{:S(2)}, u32[]{:S(2)}) %all-to-all-start) | async-done | bytes 5242912 | tf_op jit(solution)/shard_map/all_to_all | solution.py:39
  142.6 9.5 %gather_fusion = bf16[512,2560]{1,0:T(8,128)(2,1)} fusion(bf16[1024,2560]{1,0:T(8,128)(2,1)} %bitcast.5, s32[1024]{0:T(1024)S(1)} %pad_clamp_fusion), kind=kCustom, calls=%fused_computation | custom fusion | bytes 5244928 | tf_op jit(solution)/shard_map/gather | solution.py:46
  152.1 2.6 fusion.8
  154.8 4.8 %fusion.14 = f32[1280,1176]{0,1:T(8,128)} fusion(bf16[512,1176]{0,1:T(8,128)(2,1)S(1)} %copy-done.2, f32[512,1280]{1,0:T(8,128)S(1)} %get-tuple-element.15, bf16[512,2560]{1,0:T(8,128)(2,1)S(1)} %copy-done, f32[512]{0:T(512)S(1)} %get-tuple-element.16, f32[512]{0:T(512)S(1)} %get-tuple-element.17, f32[1280]{0:T(1024)S(1)} %copy-done.3, ...), kind=kOutput, calls=%fused_computation.22 | convolution fusion | flops 1548615680 | bytes 12481536 | tf_op jit(solution)/shard_map/dot_general | solution.py:68
  159.6 15.8 %concatenate.19 = f32[1280,1178]{0,1:T(8,128)} concatenate(f32[1280,1176]{0,1:T(8,128)} %fusion.14, f32[1280,1]{0,1:T(1,128)S(1)} %broadcast_in_dim.7, f32[1280,1]{0,1:T(1,128)S(1)} %broadcast_in_dim.8), dimensions={1} | concatenate | bytes 12062720 | tf_op jit(solution)/shard_map/concatenate | solution.py:74
  175.4 8.0 %copy.17 = f32[1280,1178]{1,0:T(8,128)} copy(f32[1280,1178]{0,1:T(8,128)} %concatenate.19) | data formatting | bytes 12062720
  183.4 68.2 %reduce-scatter.4.cloned.1.call-done = f32[320,1178]{1,0:T(8,128)} async-done(((f32[1280,1178]{1,0:T(8,128)}), f32[320,1178]{1,0:T(8,128)}) %reduce-scatter.4.cloned.1.call-update) | async-done | bytes 1507856
  251.6 2.8 copy.18
  254.4 187.0 %all-reduce.2.cloned.1.call-done = f32[320,1178]{0,1:T(8,128)} async-done(((f32[320,1178]{0,1:T(8,128)}), f32[320,1178]{0,1:T(8,128)}) %all-reduce.2.cloned.1.call-update) | async-done | bytes 1507856 | tf_op jit(solution)/shard_map/psum | solution.py:79
  441.4 1.5 slice-done
  442.9 1.8 copy.16
  444.7 1.3 slice_bitcast_fusion.1
  (28 shorter events, 2.0 us)
Async XLA Ops:
  16.4 10.9 %copy-start.1 = (bf16[1,1,4,3,224,224]{5,4,3,2,1,0:T(8,128)(2,1)S(1)}, bf16[1,1,4,3,224,224]{5,4,3,2,1,0:T(8,128)(2,1)}, u32[]{:S(2)}) copy-start(bf16[1,1,4,3,224,224]{5,4,3,2,1,0:T(8,128)(2,1)} %param.7) | copy-start | bytes 3612676
  16.4 126.1 %all-to-all-start = ((bf16[16,64,2560]{2,1,0:T(8,128)(2,1)}), bf16[16,64,2560]{2,1,0:T(8,128)(2,1)}, u32[]{:S(2)}, u32[]{:S(2)}) async-start(bf16[16,64,2560]{2,1,0:T(8,128)(2,1)} %bitcast.31), calls=%async_computation | async-start | bytes 10485760 | tf_op jit(solution)/shard_map/all_to_all | solution.py:39
  26.6 74.4 %all-gather.2.cloned.1.call-start = ((), (), s32[]{:S(2)}) async-start(), calls=%async_computation.2 | async-start | bytes 4096000 | tf_op jit(solution)/shard_map/all_gather | solution.py:51
  27.3 224.3 %reduce-scatter.4.cloned.1.call-start = ((), (), s32[]{:S(2)}) async-start(), calls=%async_computation.4 | async-start | bytes 8192000
  28.1 16.1 %collective-permute-start = (bf16[3,224,224]{2,1,0:T(8,128)(2,1)}, bf16[3,224,224]{2,1,0:T(8,128)(2,1)}, u32[]{:S(2)}, u32[]{:S(2)}) collective-permute-start(bf16[3,224,224]{2,1,0:T(8,128)(2,1)} %get-tuple-element.12), channel_id=1, source_target_pairs={{0,4},{4,8},{8,12},{1,5},{5,9},{9,13},{2,6},{6,10},{10,14},{3,7},{... | collective-permute-start | bytes 903176 | tf_op jit(solution)/shard_map/ppermute | solution.py:13
  36.4 7.8 %copy-start.4 = (s32[1,1,512]{2,1,0:T(1,128)S(1)}, s32[1,1,512]{2,1,0:T(1,128)}, u32[]{:S(2)}) copy-start(s32[1,1,512]{2,1,0:T(1,128)} %param.13) | copy-start | bytes 6148
  142.6 9.5 %copy-start.3 = (f32[1280]{0:T(1024)S(1)}, f32[1280]{0:T(1024)}, u32[]{:S(2)}) copy-start(f32[1280]{0:T(1024)} %param.11) | copy-start | bytes 15364
  152.1 2.7 copy-start
  152.1 2.7 copy-start.2
  183.4 258.0 %all-reduce.2.cloned.1.call-start = ((), (), s32[]{:S(2)}) async-start(), calls=%async_computation.3 | async-start | bytes 3637248 | tf_op jit(solution)/shard_map/psum | solution.py:79
  441.4 1.5 slice-start
Sparse Core Ops, SparseCore 0:
  29.2 44.2 all-gather.1
  183.5 68.0 reduce-scatter.3
  255.0 186.3 all-reduce.1
where the time goes:
time: 455 us; the launch traced here: 452 us
  waiting for transfers between devices  293 us (64%)
  local copies, waits for them, and re-layouts  101 us (22%)
  other arithmetic  22 us (5%)
  starting transfers between devices  14.1 us (3%)
  between operations  13.8 us (3%)
  matrix products  9.15 us (2%)
    psum x1, waiting for transfers between devices, shards(): summed = lax.psum(scattered, ('dp', 'slab'))  187 us
    unnamed x4, waiting for transfers between devices  68.9 us
    all_to_all x1, waiting for transfers between devices, shards(): lax.all_to_all(packed.reshape(groups, capacity, 2 * model_width), 'dp', s...  36.8 us
    transpose x1, local copies, waits for them, and re-layouts, to_rows(): ordered = jnp.transpose(split, (0, 3, 5, 2, 1, 4, 6))  24.5 us
    reshape x1, local copies, waits for them, and re-layouts, to_rows(): ordered.reshape(temporal * GH * GW, 2 * colours * patch_size * patch_size)  17.2 us
    concatenate x1, local copies, waits for them, and re-layouts, shards(): jnp.concatenate([product, gain_sum[:, None], bias_sum[:, None]], axis=1)  15.8 us
    unnamed x13, local copies, waits for them, and re-layouts  12.5 us
    all_to_all x1, starting transfers between devices, shards(): lax.all_to_all(packed.reshape(groups, capacity, 2 * model_width), 'dp', s...  10.1 us
  transfers between devices with their start and end apart: 5, of which 3 were waited for; matrix products, arithmetic and copies ran while one was open for 16% of the time, Pallas kernels for 0%

commit v1 on v0

v1 whole, which is shorter than its diff:
```python
import functools

import jax
import jax.numpy as jnp
import numpy as np
from jax import lax
from jax.experimental import pallas as pl
from jax.experimental.pallas import tpu as pltpu
from jax.sharding import Mesh
from jax.sharding import PartitionSpec as P

GH = 16
GW = 16
PS = 14
COLOURS = 3
SIDE = 224
ROWS = 512
CAP = 64
D = 1280
KIN = 1176
GROUPS = 9
PARTS = COLOURS * PS
HALF = 640
SUMS = 4 * 128 + 96
VMEM = 60 * 1024 * 1024


def column_places():
    place = np.zeros((1, KIN), np.int32)
    for c in range(COLOURS):
        for t in range(2):
            for p in range(PS):
                part = c * PS + p
                start = (1 - t) * HALF + part // GROUPS * 128 + part % GROUPS * PS
                at = (c * 2 + t) * PS * PS + p * PS
                place[0, at : at + PS] = start + np.arange(PS)
    return place


def div14(v):
    return (v * 4682) >> 16


def patch_kernel(slot_ref, fa_ref, fb_ref, out_ref, spread_ref, rows_ref):
    src = lax.broadcasted_iota(jnp.int32, (SIDE, 256), 0)
    dst = lax.broadcasted_iota(jnp.int32, (SIDE, 256), 1)
    place = jnp.where(src >= GROUPS * PS, src + 2, src)
    spread = (dst == place).astype(jnp.float32).astype(jnp.bfloat16)
    dst = lax.broadcasted_iota(jnp.int32, (SIDE, SIDE), 0)
    src = lax.broadcasted_iota(jnp.int32, (SIDE, SIDE), 1)
    regroup = (src == (dst & 15) * PS + (dst >> 4)).astype(jnp.float32).astype(jnp.bfloat16)
    for k, ref in enumerate((fa_ref, fb_ref)):
        for c in range(COLOURS):
            frame = ref[0, 0, 0, c]
            wide = jnp.dot(frame, spread, preferred_element_type=jnp.float32).astype(jnp.bfloat16)
            spread_ref[k, c] = jnp.dot(regroup, wide, preferred_element_type=jnp.float32)
    lane = lax.broadcasted_iota(jnp.int32, (GH, 128), 1)
    for k in range(2):
        for x in range(GW):
            tile = x // GROUPS * 128
            for j in range(5):
                acc = None
                used = min(GROUPS, PARTS - j * GROUPS)
                for a in range(used):
                    c, p = divmod(j * GROUPS + a, PS)
                    piece = spread_ref[k, c, p * GH : (p + 1) * GH, tile : tile + 128]
                    shift = PS * (a - x % GROUPS) % 128
                    if shift:
                        piece = pltpu.roll(piece, shift, 1)
                    acc = piece if acc is None else jnp.where(lane >= a * PS, piece, acc)
                acc = jnp.where(lane < used * PS, acc, 0.0)
                start = k * GH * GW + x * GH
                rows_ref[start : start + GH, j * 128 : (j + 1) * 128] = acc.astype(jnp.bfloat16)
    slots = slot_ref[...]

    def scatter(i, carry):
        start = pl.multiple_of(i * 256, 256)
        at = lax.broadcasted_iota(jnp.int32, (256, ROWS), 0) + start
        pick = (at == slots).astype(jnp.float32).astype(jnp.bfloat16)
        packed = jnp.dot(pick, rows_ref[...], preferred_element_type=jnp.float32)
        out_ref[pl.ds(start, 256), :] = packed.astype(jnp.bfloat16)
        return carry

    lax.fori_loop(0, 4, scatter, 0)


def packed_rows(slots, first, second, first_at, second_at):
    block = (1, 1, 1, COLOURS, SIDE, SIDE)
    return pl.pallas_call(
        patch_kernel,
        out_shape=jax.ShapeDtypeStruct((16 * CAP, HALF), jnp.bfloat16),
        grid=(1,),
        in_specs=[
            pl.BlockSpec((1, ROWS), lambda i: (0, 0)),
            pl.BlockSpec(block, lambda i: (0, 0, first_at, 0, 0, 0)),
            pl.BlockSpec(block, lambda i: (0, 0, second_at, 0, 0, 0)),
        ],
        out_specs=pl.BlockSpec((16 * CAP, HALF), lambda i: (0, 0)),
        scratch_shapes=[
            pltpu.VMEM((2, COLOURS, SIDE, 256), jnp.float32),
            pltpu.VMEM((ROWS, HALF), jnp.bfloat16),
        ],
        compiler_params=pltpu.CompilerParams(vmem_limit_bytes=VMEM),
        name="patch_rows",
    )(slots, first, second)


def weight_kernel(place_ref, w_ref, out_ref):
    place = place_ref[...]
    at = lax.broadcasted_iota(jnp.int32, (256, KIN), 0) + pl.program_id(0) * 256
    pick = (at == place).astype(jnp.float32).astype(jnp.bfloat16)
    out_ref[...] = lax.dot_general(
        pick, w_ref[...], (((1,), (1,)), ((), ())), preferred_element_type=jnp.float32
    ).astype(jnp.bfloat16)


def padded_weight(weight):
    return pl.pallas_call(
        weight_kernel,
        out_shape=jax.ShapeDtypeStruct((2 * HALF, D), jnp.bfloat16),
        grid=(5,),
        in_specs=[
            pl.BlockSpec((1, KIN), lambda i: (0, 0)),
            pl.BlockSpec((D, KIN), lambda i: (0, 0)),
        ],
        out_specs=pl.BlockSpec((256, D), lambda i: (i, 0)),
        compiler_params=pltpu.CompilerParams(vmem_limit_bytes=VMEM),
        name="weight_columns",
    )(jnp.asarray(column_places()), weight)


def backward_kernel(core_ref, slot_ref, arr0_ref, arr1_ref, w_ref, g_ref, r_ref, gain_ref, send_ref, keep_ref, rows_ref, grad_ref, sums_ref):
    gain = gain_ref[...]
    sums_ref[...] = jnp.zeros_like(sums_ref)

    def block(i, carry):
        start = pl.multiple_of(i * 128, 128)
        here = pl.ds(start, 128)
        at = lax.broadcasted_iota(jnp.int32, (128, 16 * CAP), 1)
        pick = (at == slot_ref[here, :]).astype(jnp.float32).astype(jnp.bfloat16)
        row0 = jnp.dot(pick, arr0_ref[...], preferred_element_type=jnp.float32).astype(jnp.bfloat16)
        row1 = jnp.dot(pick, arr1_ref[...], preferred_element_type=jnp.float32).astype(jnp.bfloat16)
        rows_ref[0, here, :] = row0
        rows_ref[1, here, :] = row1
        embedded = jnp.dot(row0, w_ref[:HALF, :], preferred_element_type=jnp.float32)
        embedded += jnp.dot(row1, w_ref[HALF:, :], preferred_element_type=jnp.float32)
        center = jnp.mean(embedded, axis=-1, keepdims=True)
        deviation = embedded - center
        variance = jnp.mean(deviation * deviation, axis=-1, keepdims=True)
        inverse_std = lax.rsqrt(variance + 1e-06)
        normalized = deviation * inverse_std
        upstream_norm = g_ref[0, 0, here, :].astype(jnp.float32)
        upstream = upstream_norm * gain
        inner = jnp.mean(upstream * normalized, axis=-1, keepdims=True)
        level = jnp.mean(upstream, axis=-1, keepdims=True)
        input_grad = r_ref[0, 0, here, :].astype(jnp.float32) + inverse_std * (
            upstream - level - normalized * inner
        )
        grad_ref[here, :] = input_grad.astype(jnp.bfloat16)
        sums_ref[0:1, :] += jnp.sum(upstream_norm * normalized, axis=0, keepdims=True)
        sums_ref[1:2, :] += jnp.sum(upstream_norm, axis=0, keepdims=True)
        return carry

    lax.fori_loop(0, ROWS // 128, block, 0)
    core = core_ref[0]
    lane = lax.broadcasted_iota(jnp.int32, (256, 128), 1)

    def product(i, carry):
        start = pl.multiple_of(i * 256, 256)
        here = pl.ds(start, 256)
        grads = grad_ref[:, here]
        sums = sums_ref[:, here].T
        sums = jnp.where(
            lane == SUMS % 128, sums[:, 0:1], jnp.where(lane == SUMS % 128 + 1, sums[:, 1:2], 0.0)
        )
        for half, out_ref in ((1 - core, send_ref), (core, keep_ref)):
            terms = lax.dot_general(
                grads, rows_ref[half], (((0,), (0,)), ((), ())), preferred_element_type=jnp.float32
            )
            out_ref[here, :512] = terms[:, :512].astype(out_ref.dtype)
            last = terms[:, 512:] + jnp.where(half == 0, sums, 0.0)
            out_ref[here, 512:] = last.astype(out_ref.dtype)
        return carry

    lax.fori_loop(0, D // 256, product, 0)


def products(core, slots, arr0, arr1, weight, grad_norm, grad_resid, gain):
    whole = pl.BlockSpec(memory_space=pltpu.VMEM)
    return pl.pallas_call(
        backward_kernel,
        out_shape=(
            jax.ShapeDtypeStruct((D, HALF), jnp.bfloat16),
            jax.ShapeDtypeStruct((D, HALF), jnp.float32),
        ),
        in_specs=[pl.BlockSpec(memory_space=pltpu.SMEM)] + [whole] * 7,
        out_specs=(whole, whole),
        scratch_shapes=[
            pltpu.VMEM((2, ROWS, HALF), jnp.bfloat16),
            pltpu.VMEM((ROWS, D), jnp.bfloat16),
            pltpu.VMEM((128, D), jnp.float32),
        ],
        compiler_params=pltpu.CompilerParams(vmem_limit_bytes=VMEM),
        name="norm_backward",
    )(core, slots, arr0, arr1, weight, grad_norm, grad_resid, gain)


def pieces():
    place = column_places()[0]
    runs = []
    at = 0
    while at < KIN:
        stop = at + 1
        while (
            stop < KIN
            and place[stop] == place[stop - 1] + 1
            and place[stop] % 128
            and stop % 128
        ):
            stop += 1
        runs.append((at, int(place[at]), stop - at))
        at = stop
    return runs


def finish_kernel(in_ref, out_ref, norm_ref):
    rows = in_ref.shape[1]
    lane = lax.broadcasted_iota(jnp.int32, (rows, 128), 1)
    runs = pieces()
    for tile in range(pl.cdiv(KIN, 128)):
        acc = None
        for at, src, size in runs:
            if at // 128 != tile:
                continue
            half, col = divmod(src, HALF)
            piece = in_ref[half, :, col // 128 * 128 : col // 128 * 128 + 128]
            shift = (at - src) % 128
            if shift:
                piece = pltpu.roll(piece, shift, 1)
            acc = piece if acc is None else jnp.where(lane >= at % 128, piece, acc)
        width = min(128, KIN - tile * 128)
        out_ref[:, tile * 128 : tile * 128 + width] = acc[:, :width]
    norm_ref[...] = in_ref[0, :, 512:640]


def finish(parts):
    rows = parts.shape[1]
    return pl.pallas_call(
        finish_kernel,
        out_shape=(
            jax.ShapeDtypeStruct((rows, KIN), jnp.float32),
            jax.ShapeDtypeStruct((rows, 128), jnp.float32),
        ),
        compiler_params=pltpu.CompilerParams(vmem_limit_bytes=VMEM),
        name="column_order",
    )(parts)


def shards(pixels, grad_norm, grad_resid, embed_weight, norm_gain, send_slot, recv_slot):
    core = lax.axis_index("core").astype(jnp.int32)[None]
    earlier = lax.ppermute(pixels[:, :, 3:4], "slab", [(i, i + 1) for i in range(3)])
    weight = lax.all_gather(embed_weight, "fsdp", axis=0, tiled=True)
    takes = recv_slot.reshape(2, GH, GW).transpose(0, 2, 1).reshape(1, ROWS)
    packed0 = packed_rows(takes, pixels, pixels, 0, 2)
    arrived0 = lax.all_to_all(packed0.reshape(16, CAP, HALF), ("z", "core"), 0, 0, tiled=True)
    packed1 = packed_rows(takes, earlier, pixels, 0, 1)
    arrived1 = lax.all_to_all(packed1.reshape(16, CAP, HALF), ("z", "core"), 0, 0, tiled=True)
    weight = padded_weight(weight)
    send, keep = products(
        core,
        send_slot.reshape(ROWS, 1),
        arrived0.reshape(16 * CAP, HALF),
        arrived1.reshape(16 * CAP, HALF),
        weight,
        grad_norm,
        grad_resid,
        norm_gain.reshape(1, D),
    )
    other = lax.ppermute(send, "core", [(0, 1), (1, 0)])
    pair = keep + other.astype(jnp.float32)
    spread = pair.astype(jnp.bfloat16).reshape(16, D // 16, HALF)
    plane = lax.all_to_all(spread, ("fsdp", "slab"), 0, 0, tiled=True)
    plane = jnp.sum(plane.astype(jnp.float32), axis=0)
    rows = plane.shape[0] // 8
    lines = lax.all_to_all(plane.reshape(8, rows, HALF), "z", 0, 0, tiled=True)
    line = jnp.sum(lines, axis=0, keepdims=True)
    lines = lax.all_to_all(jnp.broadcast_to(line, (8, rows, HALF)), "z", 0, 0, tiled=True)
    mine = lax.all_gather(lines.reshape(8 * rows, HALF), "slab", axis=0, tiled=True)
    both = lax.all_gather(mine, "core", axis=0)
    embed_grad, norm = finish(both)
    first = SUMS % 128
    return embed_grad, norm[:, first : first + 2].T


def solution(mesh):
    split = Mesh(mesh.devices.reshape(8, 2, 4, 4), ("z", "core", "slab", "fsdp"))
    dp = ("z", "core")
    return jax.shard_map(
        shards,
        mesh=split,
        in_specs=(
            P(dp, "fsdp", "slab", None, None, None),
            P("slab", "fsdp", dp, None),
            P("slab", "fsdp", dp, None),
            P("fsdp", None),
            P(),
            P("slab", "fsdp", dp),
            P("slab", "fsdp", dp),
        ),
        out_specs=(P("fsdp", None), P(None, "fsdp")),
        check_vma=False,
    )
```

time: 455 us -> 215 us (0.47)
  waiting for transfers between devices: 293 us -> 66.5 us
  local copies, waits for them, and re-layouts: 101 us -> 7.46 us
  blocking collectives: 0 us -> 67.1 us
  Pallas kernels: 0 us -> 38.8 us
  other arithmetic: 22 us -> 3.84 us
  matrix products: 9.15 us -> 0 us
    psum x1 -> x0, waiting for transfers between devices: 187 us -> none  [shards(): summed = lax.psum(scattered, ('dp', 'slab'))]
    unnamed x4 -> x2, waiting for transfers between devices: 68.9 us -> 0.7 us
    all_to_all x0 -> x3, blocking collectives: none -> 55.6 us  [the longest x1 29.5 us: shards(): plane = lax.all_to_all(spread, ('fsdp', 'slab'), 0, 0, tiled=True)]
    pallas_call x0 -> x5, Pallas kernels: none -> 38.8 us  [the longest x1 16.3 us: products(): pl.pallas_call(backward_kernel, out_shape=(jax.ShapeDtypeStruct((D, HALF)...]
    all_gather x1 -> x2, waiting for transfers between devices: 0.01 us -> 24.8 us  [the longest x1 16.5 us: shards(): both = lax.all_gather(mine, 'core', axis=0)]
    transpose x2 -> x1, local copies, waits for them, and re-layouts: 25.8 us -> 1.01 us  [shards(): return (embed_grad, norm[:, first:first + 2].T)]
    concatenate x3 -> x0, local copies, waits for them, and re-layouts: 24.5 us -> none  [the longest x1 15.8 us: shards(): jnp.concatenate([product, gain_sum[:, None], bias_sum[:, None]], axis=1)]
    reshape x1 -> x7, local copies, waits for them, and re-layouts: 17.2 us -> 2.35 us  [the longest x1 0.86 us: shards(): send_slot.reshape(ROWS, 1)]
  transfers between devices with their start and end apart: 5 -> 6, of which waited for: 3 -> 6; matrix products, arithmetic and copies ran while one was open for 16% -> 1% of each run, Pallas kernels for 0% -> 6%
where the time goes in v1:
time: 215 us
  blocking collectives  67.1 us (31%)
  waiting for transfers between devices  66.5 us (31%)
  Pallas kernels  38.8 us (18%)
  starting transfers between devices  17.1 us (8%)
  between operations  14.1 us (7%)
  local copies, waits for them, and re-layouts  7.46 us (3%)
  other arithmetic  3.84 us (2%)
    all_to_all x1, blocking collectives, shards(): plane = lax.all_to_all(spread, ('fsdp', 'slab'), 0, 0, tiled=True)  29.5 us
    all_gather x1, waiting for transfers between devices, shards(): both = lax.all_gather(mine, 'core', axis=0)  16.5 us
    pallas_call x1, Pallas kernels, products(): pl.pallas_call(backward_kernel, out_shape=(jax.ShapeDtypeStruct((D, HALF)...  16.3 us
    all_to_all x1, waiting for transfers between devices, shards(): lax.all_to_all(packed1.reshape(16, CAP, HALF), ('z', 'core'), 0, 0, tiled...  15.2 us
    all_to_all x1, waiting for transfers between devices, shards(): lax.all_to_all(packed0.reshape(16, CAP, HALF), ('z', 'core'), 0, 0, tiled...  14.7 us
    all_to_all x1, blocking collectives, shards(): lines = lax.all_to_all(plane.reshape(8, rows, HALF), 'z', 0, 0, tiled=True)  13.1 us
    all_to_all x1, blocking collectives, shards(): lax.all_to_all(jnp.broadcast_to(line, (8, rows, HALF)), 'z', 0, 0, tiled=...  13.1 us
    all_gather x1, blocking collectives, shards(): lax.all_gather(lines.reshape(8 * rows, HALF), 'slab', axis=0, tiled=True)  11.4 us
  transfers between devices with their start and end apart: 6, of which 6 were waited for; matrix products, arithmetic and copies ran while one was open for 1% of the time, Pallas kernels for 6%

profile of v1, /device:TPU:1, one launch (start us, length us, event | category | flops | bytes accessed | tf_op | source)
XLA Modules:
  0.0 214.8 jit_solution(8704564341640265816)
XLA Ops:
  7.7 1.3 reduce.3
  9.8 5.4 %patch_rows.2 = bf16[1024,640]{1,0:T(8,128)(2,1)} custom-call(s32[1,512]{1,0:T(1,128)} %reshape.40.slot_ref, bf16[1,1,4,3,224,224]{5,4,3,2,1,0:T(8,128)(2,1)} %fb_ref.3, bf16[1,1,4,3,224,224]{5,4,3,2,1,0:T(8,128)(2,1)} %fb_ref.3), custom_call_target="tpu_custom_call" | custom-call | tf_op jit(solution)/shard_map/patch_rows/pallas_call | solution.py:89
  15.2 10.0 %all-to-all-start = ((bf16[16,64,640]{2,1,0:T(8,128)(2,1)}), bf16[16,64,640]{2,1,0:T(8,128)(2,1)S(1)}, u32[]{:S(2)}, u32[]{:S(2)}) async-start(bf16[16,64,640]{2,1,0:T(8,128)(2,1)} %bitcast.14), calls=%async_computation | async-start | bytes 2621440 | tf_op jit(solution)/shard_map/all_to_all | solution.py:265
  26.0 1.0 slice.6
  27.0 3.2 %collective-permute-start = (bf16[1,1,1,3,224,224]{5,4,3,2,1,0:T(8,128)(2,1)S(1)}, bf16[1,1,1,3,224,224]{5,4,3,2,1,0:T(8,128)(2,1)S(1)}, u32[]{:S(2)}, u32[]{:S(2)}) collective-permute-start(bf16[1,1,1,3,224,224]{5,4,3,2,1,0:T(8,128)(2,1)S(1)} %slice.6), channel_id=1, source_target_pairs={{0,4},{4,8},{8,12},{1,5},{5,9},{9,13},{2,6},{6,10},{10,14},{3,7},{... | collective-permute-start | bytes 903176 | tf_op jit(solution)/shard_map/ppermute | solution.py:261
  30.1 7.4 %collective-permute-done.fa_ref = bf16[1,1,1,3,224,224]{5,4,3,2,1,0:T(8,128)(2,1)S(1)} collective-permute-done((bf16[1,1,1,3,224,224]{5,4,3,2,1,0:T(8,128)(2,1)S(1)}, bf16[1,1,1,3,224,224]{5,4,3,2,1,0:T(8,128)(2,1)S(1)}, u32[]{:S(2)}, u32[]{:S(2)}) %collective-permute-start) | collective-permute-done | bytes 301088 | tf_op jit(solution)/shard_map/ppermute | solution.py:261
  38.2 5.5 %patch_rows.3 = bf16[1024,640]{1,0:T(8,128)(2,1)} custom-call(s32[1,512]{1,0:T(1,128)} %reshape.40.slot_ref, bf16[1,1,1,3,224,224]{5,4,3,2,1,0:T(8,128)(2,1)} %copy-done.2, bf16[1,1,4,3,224,224]{5,4,3,2,1,0:T(8,128)(2,1)} %fb_ref.3), custom_call_target="tpu_custom_call" | custom-call | tf_op jit(solution)/shard_map/patch_rows/pallas_call | solution.py:89
  43.7 14.7 %all-to-all-done = bf16[16,64,640]{2,1,0:T(8,128)(2,1)S(1)} async-done(((bf16[16,64,640]{2,1,0:T(8,128)(2,1)}), bf16[16,64,640]{2,1,0:T(8,128)(2,1)S(1)}, u32[]{:S(2)}, u32[]{:S(2)}) %all-to-all-start) | async-done | bytes 1310752 | tf_op jit(solution)/shard_map/all_to_all | solution.py:265
  58.4 3.9 %all-to-all-start.1 = ((bf16[16,64,640]{2,1,0:T(8,128)(2,1)}), bf16[16,64,640]{2,1,0:T(8,128)(2,1)S(1)}, u32[]{:S(2)}, u32[]{:S(2)}) async-start(bf16[16,64,640]{2,1,0:T(8,128)(2,1)} %bitcast.15), calls=%async_computation.1 | async-start | bytes 2621440 | tf_op jit(solution)/shard_map/all_to_all | solution.py:267
  63.0 0.9 copy.13.slot_ref
  63.8 8.3 %all-gather.4.cloned.1.call-done.w_ref = bf16[1280,1176]{1,0:T(8,128)(2,1)} async-done(((bf16[320,1176]{1,0:T(8,128)(2,1)}), bf16[1280,1176]{1,0:T(8,128)(2,1)}) %all-gather.4.cloned.1.call-update) | async-done | bytes 3010576 | tf_op jit(solution)/shard_map/all_gather | solution.py:262
  72.2 8.1 %weight_columns.1.w_ref = bf16[1280,1280]{1,0:T(8,128)(2,1)} custom-call(s32[1,1176]{1,0:T(1,128)} %constant.10.clone.place_ref, bf16[1280,1176]{1,0:T(8,128)(2,1)} %all-gather.4.cloned.1.call-done.w_ref), custom_call_target="tpu_custom_call" | custom-call | tf_op jit(solution)/shard_map/weight_columns/pallas_call | solution.py:118
  80.3 15.2 %all-to-all-done.1 = bf16[16,64,640]{2,1,0:T(8,128)(2,1)S(1)} async-done(((bf16[16,64,640]{2,1,0:T(8,128)(2,1)}), bf16[16,64,640]{2,1,0:T(8,128)(2,1)S(1)}, u32[]{:S(2)}, u32[]{:S(2)}) %all-to-all-start.1) | async-done | bytes 1310752 | tf_op jit(solution)/shard_map/all_to_all | solution.py:267
  95.5 1.1 copy-done.1
  96.6 16.3 %norm_backward.1 = (bf16[1280,640]{1,0:T(8,128)(2,1)}, f32[1280,640]{1,0:T(8,128)}) custom-call(s32[1]{0:T(128)} %bitcast.core_ref, s32[512,1]{1,0:T(8,128)} %copy.13.slot_ref, bf16[1024,640]{1,0:T(8,128)(2,1)} %bitcast.12, bf16[1024,640]{1,0:T(8,128)(2,1)} %bitcast.13, bf16[1280,1280]{1,0:T(8,128)(2,1)} %weight_columns.1.w_ref, ...), custom_call_target="tpu_custom_call" | custom-call | tf_op jit(solution)/shard_map/norm_backward/pallas_call | solution.py:190
  112.9 3.7 %collective-permute-done.1 = bf16[1280,640]{1,0:T(8,128)(2,1)S(1)} collective-permute-done((bf16[1280,640]{1,0:T(8,128)(2,1)}, bf16[1280,640]{1,0:T(8,128)(2,1)S(1)}, u32[]{:S(2)}, u32[]{:S(2)}) %collective-permute-start.1) | collective-permute-done | bytes 1638432 | tf_op jit(solution)/shard_map/ppermute | solution.py:279
  116.6 2.2 %add_convert_fusion = bf16[1280,640]{1,0:T(8,128)(2,1)S(1)} fusion(f32[1280,640]{1,0:T(8,128)} %get-tuple-element.6, bf16[1280,640]{1,0:T(8,128)(2,1)S(1)} %collective-permute-done.1), kind=kLoop, calls=%fused_computation.1 | loop fusion | flops 2457600 | bytes 6553600 | tf_op jit(solution)/shard_map/convert_element_type | solution.py:281
  118.9 29.5 %all_to_all.25 = bf16[16,80,640]{2,1,0:T(8,128)(2,1)S(1)} all-to-all(bf16[16,80,640]{2,1,0:T(8,128)(2,1)S(1)} %bitcast.11), channel_id=1, replica_groups=mesh['z'=8,'core'=2,'slab'=4,'fsdp'=4] {'fsdp','slab'}, dimensions={0} | all-to-all | bytes 3276800 | tf_op jit(solution)/shard_map/all_to_all | solution.py:282
  148.6 13.1 %all_to_all.26 = f32[8,10,640]{2,1,0:T(8,128)S(1)} all-to-all(f32[8,10,640]{2,1,0:T(8,128)S(1)} %reshape.47), channel_id=1, replica_groups=mesh['z'=8,'core'=2,'slab'=4,'fsdp'=4] {'z'}, dimensions={0} | all-to-all | bytes 409600 | tf_op jit(solution)/shard_map/all_to_all | solution.py:285
  161.8 13.1 %all_to_all.27 = f32[8,10,640]{2,1,0:T(8,128)S(1)} all-to-all(f32[8,10,640]{2,1,0:T(8,128)S(1)} %broadcast_in_dim.10), channel_id=1, replica_groups=mesh['z'=8,'core'=2,'slab'=4,'fsdp'=4] {'z'}, dimensions={0} | all-to-all | bytes 409600 | tf_op jit(solution)/shard_map/all_to_all | solution.py:287
  174.8 11.4 %all_gather.13 = f32[320,640]{1,0:T(8,128)} all-gather(f32[80,640]{1,0:T(8,128)S(1)} %reshape.48), channel_id=1, replica_groups=mesh['z'=8,'core'=2,'slab'=4,'fsdp'=4] {'slab'}, dimensions={0}, use_global_device_ids=true | all-gather | bytes 1024000 | tf_op jit(solution)/shard_map/all_gather | solution.py:288
  186.3 16.5 %all-gather.6.cloned.1.call-done = f32[640,640]{1,0:T(8,128)} async-done(((f32[320,640]{1,0:T(8,128)}), f32[640,640]{1,0:T(8,128)}) %all-gather.6.cloned.1.call-update) | async-done | bytes 1638416 | tf_op jit(solution)/shard_map/all_gather | solution.py:289
  202.8 3.5 %column_order.1 = (f32[320,1176]{1,0:T(8,128)}, f32[320,128]{1,0:T(8,128)}) custom-call(f32[2,320,640]{2,1,0:T(8,128)} %bitcast.16), custom_call_target="tpu_custom_call" | custom-call | tf_op jit(solution)/shard_map/column_order/pallas_call | solution.py:248
  206.3 1.0 slice_bitcast_fusion
  (25 shorter events, 4.5 us)
Async XLA Ops:
  15.2 43.2 %all-to-all-start = ((bf16[16,64,640]{2,1,0:T(8,128)(2,1)}), bf16[16,64,640]{2,1,0:T(8,128)(2,1)S(1)}, u32[]{:S(2)}, u32[]{:S(2)}) async-start(bf16[16,64,640]{2,1,0:T(8,128)(2,1)} %bitcast.14), calls=%async_computation | async-start | bytes 2621440 | tf_op jit(solution)/shard_map/all_to_all | solution.py:265
  25.2 46.9 %all-gather.4.cloned.1.call-start = ((), (), s32[]{:S(2)}) async-start(), calls=%async_computation.5 | async-start | bytes 4096000 | tf_op jit(solution)/shard_map/all_gather | solution.py:262
  27.0 10.5 %collective-permute-start = (bf16[1,1,1,3,224,224]{5,4,3,2,1,0:T(8,128)(2,1)S(1)}, bf16[1,1,1,3,224,224]{5,4,3,2,1,0:T(8,128)(2,1)S(1)}, u32[]{:S(2)}, u32[]{:S(2)}) collective-permute-start(bf16[1,1,1,3,224,224]{5,4,3,2,1,0:T(8,128)(2,1)S(1)} %slice.6), channel_id=1, source_target_pairs={{0,4},{4,8},{8,12},{1,5},{5,9},{9,13},{2,6},{6,10},{10,14},{3,7},{... | collective-permute-start | bytes 903176 | tf_op jit(solution)/shard_map/ppermute | solution.py:261
  37.5 0.7 copy-start.2
  43.7 18.7 %copy-start.3 = (f32[1280]{0:T(1024)S(1)}, f32[1280]{0:T(1024)}, u32[]{:S(2)}) copy-start(f32[1280]{0:T(1024)} %param.12) | copy-start | bytes 15364
  43.7 19.3 %copy-start.4 = (s32[1,1,512]{2,1,0:T(1,128)S(1)}, s32[1,1,512]{2,1,0:T(1,128)}, u32[]{:S(2)}) copy-start(s32[1,1,512]{2,1,0:T(1,128)} %param.13) | copy-start | bytes 6148
  58.4 21.9 %copy-start = (bf16[16,64,640]{2,1,0:T(8,128)(2,1)}, bf16[16,64,640]{2,1,0:T(8,128)(2,1)S(1)}, u32[]{:S(2)}) copy-start(bf16[16,64,640]{2,1,0:T(8,128)(2,1)S(1)} %all-to-all-done) | copy-start | bytes 3932164
  58.4 37.1 %all-to-all-start.1 = ((bf16[16,64,640]{2,1,0:T(8,128)(2,1)}), bf16[16,64,640]{2,1,0:T(8,128)(2,1)S(1)}, u32[]{:S(2)}, u32[]{:S(2)}) async-start(bf16[16,64,640]{2,1,0:T(8,128)(2,1)} %bitcast.15), calls=%async_computation.1 | async-start | bytes 2621440 | tf_op jit(solution)/shard_map/all_to_all | solution.py:267
  62.3 140.5 %all-gather.6.cloned.1.call-start = ((), (), s32[]{:S(2)}) async-start(), calls=%async_computation.6 | async-start | bytes 2457600 | tf_op jit(solution)/shard_map/all_gather | solution.py:289
  95.5 1.1 copy-start.1
  112.9 3.7 %collective-permute-start.1 = (bf16[1280,640]{1,0:T(8,128)(2,1)}, bf16[1280,640]{1,0:T(8,128)(2,1)S(1)}, u32[]{:S(2)}, u32[]{:S(2)}) collective-permute-start(bf16[1280,640]{1,0:T(8,128)(2,1)} %get-tuple-element.7), channel_id=1, source_target_pairs={{0,16},{16,0},{1,17},{17,1},{2,18},{18,2},{3,19},{19,3},{4,20},{20... | collective-permute-start | bytes 4915208 | tf_op jit(solution)/shard_map/ppermute | solution.py:279
Sparse Core Ops, SparseCore 0:
  27.9 44.2 all-gather.3
  186.4 16.2 all-gather.5

commit v2 on v1

v2 whole, which is shorter than its diff:
```python
import jax
import jax.numpy as jnp
import numpy as np
from jax import lax
from jax.experimental import pallas as pl
from jax.experimental.pallas import tpu as pltpu
from jax.sharding import Mesh
from jax.sharding import PartitionSpec as P

GH = 16
GW = 16
PS = 14
COLOURS = 3
SIDE = 224
ROWS = 512
CAP = 64
PEERS = 16
D = 1280
KIN = 1176
GROUPS = 9
PARTS = COLOURS * PS
FRAME = PARTS * PS
SPLIT = FRAME // 2
HELD = 296
SECOND = 304
HALF = 640
TILES = HALF // 128
OWNED = D // 4
LINE = OWNED * TILES
QUARTER = LINE // 4
STEP = 80
PIECE = 56
SUMS = 96
VMEM = 60 * 1024 * 1024
ALL = pl.BlockSpec(memory_space=pltpu.VMEM)
SCALAR = pl.BlockSpec(memory_space=pltpu.SMEM)
PARAMS = pltpu.CompilerParams(vmem_limit_bytes=VMEM)
LANES = (((1,), (1,)), ((), ()))
SUBLANES = (((0,), (0,)), ((), ()))


def one_hot(match):
    return match.astype(jnp.float32).astype(jnp.bfloat16)


def iota(shape, dim):
    return lax.broadcasted_iota(jnp.int32, shape, dim)


def dot(a, b, dims=(((1,), (0,)), ((), ()))):
    return lax.dot_general(a, b, dims, preferred_element_type=jnp.float32)


def column_places():
    place = np.zeros((1, KIN), np.int32)
    for c in range(COLOURS):
        for t in range(2):
            part = c * PS * PS + np.arange(PS * PS)
            at = (c * 2 + t) * PS * PS
            place[0, at : at + PS * PS] = (1 - t) * HALF + part + np.where(part >= SPLIT, SECOND - SPLIT, 0)
    return place


def patch_kernel(valid_ref, slot_ref, fa_ref, fb_ref, out_ref, spread_ref, rows_ref, low_ref, high_ref):
    src = iota((SIDE, 256), 0)
    place = jnp.where(src >= GROUPS * PS, src + 2, src)
    spread = one_hot(iota((SIDE, 256), 1) == place)
    dst = iota((SIDE, SIDE), 0)
    regroup = one_hot(iota((SIDE, SIDE), 1) == (dst & 15) * PS + (dst >> 4))
    for k, ref in enumerate((fa_ref, fb_ref)):
        for c in range(COLOURS):
            frame = ref[0, 0, 0, c]
            wide = dot(frame, spread).astype(jnp.bfloat16)
            spread_ref[k, c] = dot(regroup, wide)

    @pl.when(valid_ref[0] == 0)
    def _():
        spread_ref[0] = jnp.zeros_like(spread_ref[0])

    lane = iota((GH, 128), 1)
    for k in range(2):
        for x in range(GW):
            tile = x // GROUPS * 128
            for j in range(TILES):
                acc = None
                used = min(GROUPS, PARTS - j * GROUPS)
                for a in range(used):
                    c, p = divmod(j * GROUPS + a, PS)
                    piece = spread_ref[k, c, p * GH : (p + 1) * GH, tile : tile + 128]
                    shift = PS * (a - x % GROUPS) % 128
                    if shift:
                        piece = pltpu.roll(piece, shift, 1)
                    acc = piece if acc is None else jnp.where(lane >= a * PS, piece, acc)
                acc = jnp.where(lane < used * PS, acc, 0.0)
                start = k * GH * GW + x * GH
                rows_ref[start : start + GH, j * 128 : (j + 1) * 128] = acc.astype(jnp.bfloat16)
    row = iota((SECOND, HALF), 0)
    column = iota((SECOND, HALF), 1)
    for begin, ref in ((0, low_ref), (SPLIT, high_ref)):
        value = row + begin
        gaps = sum((value >= n * GROUPS * PS).astype(jnp.int32) for n in range(1, TILES))
        pick = one_hot((column == value + 2 * gaps) & (row < SPLIT))
        ref[...] = dot(pick, rows_ref[...], LANES).astype(jnp.bfloat16)
    slots = slot_ref[...]
    kind = iota((16, ROWS), 0)
    digits = jnp.where(kind == 0, slots >> 6, jnp.where(kind == 1, slots & 63, 0))
    dst = iota((ROWS, ROWS), 0)
    order = one_hot(iota((ROWS, ROWS), 1) == (dst & 256) + ((dst & 15) << 4) + ((dst >> 4) & 15))
    digits = dot(order, digits.astype(jnp.float32).astype(jnp.bfloat16), LANES)
    slots = (digits[:, 0:1] * 64.0 + digits[:, 1:2]).astype(jnp.int32)
    side = iota((HELD, 128), 1) < CAP
    for i in range(PEERS // 4):
        pick = one_hot(iota((ROWS, 256), 1) + i * 256 == slots)
        low = dot(low_ref[...], pick)[:HELD]
        high = dot(high_ref[...], pick)[:HELD]
        for j in range(2):
            lo = low[:, j * 128 : (j + 1) * 128]
            hi = high[:, j * 128 : (j + 1) * 128]
            peer = i * 4 + j * 2
            out_ref[peer] = jnp.where(side, lo, pltpu.roll(hi, CAP, 1)).astype(jnp.bfloat16)
            out_ref[peer + 1] = jnp.where(side, pltpu.roll(lo, CAP, 1), hi).astype(jnp.bfloat16)


def packed_rows(valid, slots, first, second, first_at, second_at):
    block = (1, 1, 1, COLOURS, SIDE, SIDE)
    shape = (PEERS, HELD, 128)
    return pl.pallas_call(
        patch_kernel,
        out_shape=jax.ShapeDtypeStruct(shape, jnp.bfloat16),
        grid=(1,),
        in_specs=[
            SCALAR,
            pl.BlockSpec((1, ROWS), lambda i: (0, 0)),
            pl.BlockSpec(block, lambda i: (0, 0, first_at, 0, 0, 0)),
            pl.BlockSpec(block, lambda i: (0, 0, second_at, 0, 0, 0)),
        ],
        out_specs=pl.BlockSpec(shape, lambda i: (0, 0, 0)),
        scratch_shapes=[
            pltpu.VMEM((2, COLOURS, SIDE, 256), jnp.float32),
            pltpu.VMEM((ROWS, HALF), jnp.bfloat16),
            pltpu.VMEM((SECOND, ROWS), jnp.bfloat16),
            pltpu.VMEM((SECOND, ROWS), jnp.bfloat16),
        ],
        compiler_params=PARAMS,
        name="patch_rows",
    )(valid, slots, first, second)


def weight_kernel(place_ref, w_ref, out_ref):
    at = iota((256, KIN), 0) + pl.program_id(0) * 256
    pick = one_hot(at == place_ref[...])
    out_ref[...] = dot(pick, w_ref[...], LANES).astype(jnp.bfloat16)


def padded_weight(weight):
    return pl.pallas_call(
        weight_kernel,
        out_shape=jax.ShapeDtypeStruct((2 * HALF, D), jnp.bfloat16),
        grid=(5,),
        in_specs=[
            pl.BlockSpec((1, KIN), lambda i: (0, 0)),
            pl.BlockSpec((D, KIN), lambda i: (0, 0)),
        ],
        out_specs=pl.BlockSpec((256, D), lambda i: (i, 0)),
        compiler_params=PARAMS,
        name="weight_columns",
    )(jnp.asarray(column_places()), weight)


def taken_rows(slot_ref, arr_ref, cols_ref):
    side = iota((HELD, 128), 1) < CAP
    gap = jnp.zeros((SECOND - HELD, 128), jnp.float32)
    for j in range(PEERS // 2):
        even = arr_ref[2 * j].astype(jnp.float32)
        odd = arr_ref[2 * j + 1].astype(jnp.float32)
        low = jnp.where(side, even, pltpu.roll(odd, CAP, 1))
        high = jnp.where(side, pltpu.roll(even, CAP, 1), odd)
        at = slice(j * 128, (j + 1) * 128)
        cols_ref[0:SECOND, at] = jnp.concatenate([low, gap], axis=0).astype(jnp.bfloat16)
        cols_ref[SECOND : 2 * SECOND, at] = jnp.concatenate([high, gap], axis=0).astype(jnp.bfloat16)
    cols_ref[2 * SECOND :, :] = jnp.zeros((HALF - 2 * SECOND, PEERS * CAP), jnp.bfloat16)
    pick = one_hot(iota((ROWS, PEERS * CAP), 1) == slot_ref[...])
    return dot(pick, cols_ref[...], LANES).astype(jnp.bfloat16)


def first_kernel(slot_ref, arr_ref, w_ref, rows_ref, part_ref, cols_ref):
    rows_ref[...] = taken_rows(slot_ref, arr_ref, cols_ref)

    def block(i, carry):
        here = pl.ds(pl.multiple_of(i * 128, 128), 128)
        part_ref[here, :] = dot(rows_ref[here, :], w_ref[...])
        return carry

    lax.fori_loop(0, ROWS // 128, block, 0)


def first_half(slots, arrived, weight):
    return pl.pallas_call(
        first_kernel,
        out_shape=(
            jax.ShapeDtypeStruct((ROWS, HALF), jnp.bfloat16),
            jax.ShapeDtypeStruct((ROWS, D), jnp.float32),
        ),
        grid=(1,),
        in_specs=[
            pl.BlockSpec((ROWS, 1), lambda i: (0, 0)),
            pl.BlockSpec((PEERS, HELD, 128), lambda i: (0, 0, 0)),
            pl.BlockSpec((HALF, D), lambda i: (0, 0)),
        ],
        out_specs=(pl.BlockSpec((ROWS, HALF), lambda i: (0, 0)), pl.BlockSpec((ROWS, D), lambda i: (0, 0))),
        scratch_shapes=[pltpu.VMEM((HALF, PEERS * CAP), jnp.bfloat16)],
        compiler_params=PARAMS,
        name="first_half",
    )(slots, arrived, weight)


def second_kernel(core_ref, slot_ref, arr_ref, rows0_ref, rows1_ref, mine_ref, send_ref, cols_ref):
    rows1 = taken_rows(slot_ref, arr_ref, cols_ref)
    rows1_ref[...] = rows1

    @pl.when(core_ref[0] == 0)
    def _():
        mine_ref[...] = rows0_ref[...]
        send_ref[...] = rows1

    @pl.when(core_ref[0] != 0)
    def _():
        mine_ref[...] = rows1
        send_ref[...] = rows0_ref[...]


def second_half(core, slots, arrived, rows0):
    half = jax.ShapeDtypeStruct((ROWS, HALF), jnp.bfloat16)
    return pl.pallas_call(
        second_kernel,
        out_shape=(half, half, half),
        in_specs=[SCALAR, ALL, ALL, ALL],
        out_specs=(ALL, ALL, ALL),
        scratch_shapes=[pltpu.VMEM((HALF, PEERS * CAP), jnp.bfloat16)],
        compiler_params=PARAMS,
        name="second_half",
    )(core, slots, arrived, rows0)


def norm_kernel(rows_ref, part_ref, w_ref, g_ref, r_ref, gain_ref, grad_ref, sums_ref, embedded_ref):
    @pl.when(pl.program_id(0) == 0)
    def _():
        sums_ref[...] = jnp.zeros_like(sums_ref)

    embedded_ref[...] = part_ref[...] + dot(rows_ref[...], w_ref[...])
    gain = gain_ref[...]

    def block(i, carry):
        here = pl.ds(pl.multiple_of(i * 16, 16), 16)
        embedded = embedded_ref[here, :]
        deviation = embedded - jnp.mean(embedded, axis=-1, keepdims=True)
        variance = jnp.mean(deviation * deviation, axis=-1, keepdims=True)
        inverse_std = lax.rsqrt(variance + 1e-06)
        normalized = deviation * inverse_std
        upstream_norm = g_ref[0, 0, here, :].astype(jnp.float32)
        upstream = upstream_norm * gain
        inner = jnp.mean(upstream * normalized, axis=-1, keepdims=True)
        level = jnp.mean(upstream, axis=-1, keepdims=True)
        input_grad = r_ref[0, 0, here, :].astype(jnp.float32) + inverse_std * (
            upstream - level - normalized * inner
        )
        grad_ref[here, :] = input_grad.astype(jnp.bfloat16)
        gain_terms = upstream_norm * normalized
        sums_ref[0:8, :] += gain_terms[0:8] + gain_terms[8:16]
        sums_ref[8:16, :] += upstream_norm[0:8] + upstream_norm[8:16]
        return carry

    lax.fori_loop(0, 8, block, 0)


def norm_backward(rows, part, weight, grad_norm, grad_resid, gain):
    packed = pl.BlockSpec((1, 1, 128, D), lambda i: (0, 0, i, 0))
    return pl.pallas_call(
        norm_kernel,
        out_shape=(
            jax.ShapeDtypeStruct((ROWS, D), jnp.bfloat16),
            jax.ShapeDtypeStruct((16, D), jnp.float32),
        ),
        grid=(ROWS // 128,),
        in_specs=[
            pl.BlockSpec((128, HALF), lambda i: (i, 0)),
            pl.BlockSpec((128, D), lambda i: (i, 0)),
            pl.BlockSpec((HALF, D), lambda i: (1, 0)),
            packed,
            packed,
            pl.BlockSpec((1, D), lambda i: (0, 0)),
        ],
        out_specs=(pl.BlockSpec((128, D), lambda i: (i, 0)), pl.BlockSpec((16, D), lambda i: (0, 0))),
        scratch_shapes=[pltpu.VMEM((128, D), jnp.float32)],
        compiler_params=PARAMS,
        name="norm_backward",
    )(rows, part, weight, grad_norm, grad_resid, gain)


def product_kernel(core_ref, grad0_ref, grad1_ref, rows0_ref, rows1_ref, sums_ref, own_ref, send_ref, terms_ref):
    core, place = core_ref[0], core_ref[1]
    kind = iota((128, HALF), 0)
    lane = iota((HALF, 128), 1)
    for i in range(D // HALF):
        here = slice(i * HALF, (i + 1) * HALF)
        terms_ref[...] = dot(grad0_ref[:, here], rows0_ref[...], SUBLANES)
        terms_ref[...] += dot(grad1_ref[:, here], rows1_ref[...], SUBLANES)
        gain_sum = jnp.sum(sums_ref[0:8, here], axis=0, keepdims=True)
        bias_sum = jnp.sum(sums_ref[8:16, here], axis=0, keepdims=True)
        sums = jnp.where(kind == SUMS, gain_sum, jnp.where(kind == SUMS + 1, bias_sum, 0.0))
        terms_ref[:, HALF - 128 :] += sums.T
        for n in range(HALF // STEP):
            y, r = divmod(i * (HALF // STEP) + n, OWNED // STEP)
            for t in range(TILES):
                o = t * (OWNED // STEP) + r
                block = terms_ref[n * STEP : (n + 1) * STEP, t * 128 : (t + 1) * 128]
                to = jnp.where(core == 0, y, o // 5)
                at = jnp.where(core == 0, o * STEP, y * QUARTER + o % 5 * STEP)
                at = pl.ds(pl.multiple_of(at, 16), STEP)
                by = (to - place) & 3

                @pl.when(by == 0)
                def _():
                    own_ref[at, :] = block

                @pl.when(by != 0)
                def _():
                    send_ref[jnp.maximum(by - 1, 0), at, :] = block.astype(jnp.bfloat16)


def products(core, grad0, grad1, rows0, rows1, sums):
    return pl.pallas_call(
        product_kernel,
        out_shape=(
            jax.ShapeDtypeStruct((LINE, 128), jnp.float32),
            jax.ShapeDtypeStruct((3, LINE, 128), jnp.bfloat16),
        ),
        in_specs=[SCALAR] + [ALL] * 5,
        out_specs=(ALL, ALL),
        scratch_shapes=[pltpu.VMEM((HALF, HALF), jnp.float32)],
        compiler_params=PARAMS,
        name="products",
    )(core, grad0, grad1, rows0, rows1, sums)


def runs():
    place = column_places()[0]
    found = []
    at = 0
    while at < KIN:
        stop = at + 1
        while stop < KIN and place[stop] == place[stop - 1] + 1 and place[stop] % 128 and stop % 128:
            stop += 1
        found.append((at, int(place[at]), stop - at))
        at = stop
    return found


def finish_kernel(core_ref, mine_ref, other_ref, out_ref, norm_ref, held_ref, last_ref):
    here = core_ref[0] == 0
    for t in range(TILES):
        for r in range(OWNED // STEP):
            x, w = divmod(t * (OWNED // STEP) + r, 5)
            mine = mine_ref[x, w * STEP : (w + 1) * STEP, :]
            other = other_ref[x, w * STEP : (w + 1) * STEP, :]
            at = slice(r * STEP, (r + 1) * STEP)
            held_ref[t, at, :] = jnp.where(here, mine, other)
            held_ref[TILES + t, at, :] = jnp.where(here, other, mine)
    lane = iota((OWNED, 128), 1)
    for tile in range(pl.cdiv(KIN, 128)):
        acc = None
        for at, src, size in runs():
            if at // 128 != tile:
                continue
            piece = held_ref[src // 128]
            shift = (at - src) % 128
            if shift:
                piece = pltpu.roll(piece, shift, 1)
            acc = piece if acc is None else jnp.where(lane >= at % 128, piece, acc)
        width = min(128, KIN - tile * 128)
        out_ref[:, tile * 128 : tile * 128 + width] = acc[:, :width]
    last_ref[0:OWNED, :] = held_ref[TILES - 1] + held_ref[2 * TILES - 1]
    last_ref[OWNED:, :] = jnp.zeros((384 - OWNED, 128), jnp.float32)
    norm_ref[...] = last_ref[...].T[SUMS : SUMS + 2, :OWNED]


def finish(core, mine, other):
    return pl.pallas_call(
        finish_kernel,
        out_shape=(
            jax.ShapeDtypeStruct((OWNED, KIN), jnp.float32),
            jax.ShapeDtypeStruct((2, OWNED), jnp.float32),
        ),
        in_specs=[SCALAR, ALL, ALL],
        out_specs=(ALL, ALL),
        scratch_shapes=[
            pltpu.VMEM((2 * TILES, OWNED, 128), jnp.float32),
            pltpu.VMEM((384, 128), jnp.float32),
        ],
        compiler_params=PARAMS,
        name="column_order",
    )(core, mine, other)


def plane_index(core, x, y):
    return (core * 4 + x) * 4 + y


def plane_shift(by):
    pairs = []
    for x in range(4):
        for y in range(4):
            pairs.append((plane_index(0, x, y), plane_index(0, x, (y + by) % 4)))
            pairs.append((plane_index(1, x, y), plane_index(1, (x + by) % 4, y)))
    return pairs


def copies(array, axis, count):
    array = jnp.broadcast_to(array[None], (count,) + array.shape)
    return lax.all_to_all(array, axis, 0, 0, tiled=True)


def shards(pixels, grad_norm, grad_resid, embed_weight, norm_gain, send_slot, recv_slot):
    plane = ("core", "slab", "fsdp")
    core = lax.axis_index("core").astype(jnp.int32)
    x = lax.axis_index("slab").astype(jnp.int32)
    y = lax.axis_index("fsdp").astype(jnp.int32)
    place = jnp.stack([core, jnp.where(core == 0, y, x)])
    earlier = lax.ppermute(pixels[:, :, 3:4], "slab", [(i, (i + 1) % 4) for i in range(4)])
    weight = lax.all_gather(embed_weight, "fsdp", axis=0, tiled=True)
    takes = recv_slot.reshape(1, ROWS)
    sends = send_slot.reshape(ROWS, 1)
    packed0 = packed_rows(jnp.ones((1,), jnp.int32), takes, pixels, pixels, 0, 2)
    arrived0 = lax.all_to_all(packed0, ("z", "core"), 0, 0, tiled=True)
    packed1 = packed_rows((x > 0).astype(jnp.int32)[None], takes, earlier, pixels, 0, 1)
    arrived1 = lax.all_to_all(packed1, ("z", "core"), 0, 0, tiled=True)
    weight = padded_weight(weight)
    rows0, part = first_half(sends, arrived0, weight)
    rows1, mine, send = second_half(place, sends, arrived1, rows0)
    swap = [(0, 1), (1, 0)]
    theirs = lax.ppermute(send, "core", swap)
    grads, sums = norm_backward(rows1, part, weight, grad_norm, grad_resid, norm_gain.reshape(1, D))
    their_grads = lax.ppermute(grads, "core", swap)
    own, sent = products(place, grads, their_grads, mine, theirs, sums)
    terms = [lax.ppermute(sent[by - 1], plane, plane_shift(by)) for by in (1, 3, 2)]
    line = own + terms[0].astype(jnp.float32) + terms[1].astype(jnp.float32) + terms[2].astype(jnp.float32)
    across = [[plane_index(0, i, j) for i in range(4)] for j in range(4)]
    across += [[plane_index(1, i, j) for j in range(4)] for i in range(4)]
    quarters = lax.all_to_all(
        line.reshape(4, QUARTER, 128), plane, 0, 0, tiled=True, axis_index_groups=across
    )
    quarter = jnp.pad(jnp.sum(quarters, axis=0), ((0, 8 * PIECE - QUARTER), (0, 0)))
    pieces = lax.all_to_all(quarter.reshape(8, PIECE, 128), "z", 0, 0, tiled=True)
    quarter = copies(jnp.sum(pieces, axis=0), "z", 8).reshape(8 * PIECE, 128)
    line = copies(quarter, "slab", 4)
    return finish(place, line, lax.ppermute(line, "core", swap))


def solution(mesh):
    split = Mesh(mesh.devices.reshape(8, 2, 4, 4), ("z", "core", "slab", "fsdp"))
    dp = ("z", "core")
    return jax.shard_map(
        shards,
        mesh=split,
        in_specs=(
            P(dp, "fsdp", "slab", None, None, None),
            P("slab", "fsdp", dp, None),
            P("slab", "fsdp", dp, None),
            P("fsdp", None),
            P(),
            P("slab", "fsdp", dp),
            P("slab", "fsdp", dp),
        ),
        out_specs=(P("fsdp", None), P(None, "fsdp")),
        check_vma=False,
    )
```

time: 215 us -> 204 us (0.949)
  blocking collectives: 67.1 us -> 47.8 us
  Pallas kernels: 38.8 us -> 55 us
  waiting for transfers between devices: 66.5 us -> 51.9 us
  starting transfers between devices: 17.1 us -> 25.8 us
  other arithmetic: 3.84 us -> 0.88 us
    all_gather x1 -> x0, waiting for transfers between devices: 16.5 us -> none  [shards(): both = lax.all_gather(mine, 'core', axis=0)]
    pallas_call x4 -> x7, Pallas kernels: 30.6 us -> 46.8 us  [the longest x1 14 us: norm_backward(): pl.pallas_call(norm_kernel, out_shape=(jax.ShapeDtypeStruct((ROWS, D), jn...]
    ppermute x2 -> x7, waiting for transfers between devices: 11.1 us -> 24.7 us  [the longest x1 9.6 us: shards(): lax.ppermute(pixels[:, :, 3:4], 'slab', [(i, (i + 1) % 4) for i in range(...]
    all_to_all x2, waiting for transfers between devices: 29.9 us -> 16.7 us  [the longest x1 12 us: shards(): arrived0 = lax.all_to_all(packed0, ('z', 'core'), 0, 0, tiled=True)]
    all_gather x1 -> x0, blocking collectives: 11.4 us -> none  [shards(): lax.all_gather(lines.reshape(8 * rows, HALF), 'slab', axis=0, tiled=True)]
    ppermute x2 -> x7, starting transfers between devices: 3.16 us -> 12 us  [the longest x1 5.9 us: shards(): return finish(place, line, lax.ppermute(line, 'core', swap))]
    all_to_all x3 -> x4, blocking collectives: 55.6 us -> 47.8 us  [the longest x2 23.3 us: copies(): return lax.all_to_all(array, axis, 0, 0, tiled=True)]
    convert_element_type x1 -> x0, other arithmetic: 2.24 us -> none  [shards(): spread = pair.astype(jnp.bfloat16).reshape(16, D // 16, HALF)]
  transfers between devices with their start and end apart: 6 -> 10, of which waited for: 6 -> 9; matrix products, arithmetic and copies ran while one was open for 1% -> 2% of each run, Pallas kernels for 6% -> 10%
where the time goes in v2:
time: 204 us; the launch traced here: 203 us
  Pallas kernels  55 us (27%)
  waiting for transfers between devices  51.9 us (25%)
  blocking collectives  47.8 us (23%)
  starting transfers between devices  25.8 us (13%)
  between operations  14.1 us (7%)
  local copies, waits for them, and re-layouts  7.89 us (4%)
    all_to_all x2, blocking collectives, copies(): return lax.all_to_all(array, axis, 0, 0, tiled=True)  23.3 us
    pallas_call x1, Pallas kernels, norm_backward(): pl.pallas_call(norm_kernel, out_shape=(jax.ShapeDtypeStruct((ROWS, D), jn...  14 us
    all_to_all x1, blocking collectives, shards(): lax.all_to_all(line.reshape(4, QUARTER, 128), plane, 0, 0, tiled=True, ax...  12.3 us
    all_to_all x1, blocking collectives, shards(): lax.all_to_all(quarter.reshape(8, PIECE, 128), 'z', 0, 0, tiled=True)  12.1 us
    all_to_all x1, waiting for transfers between devices, shards(): arrived0 = lax.all_to_all(packed0, ('z', 'core'), 0, 0, tiled=True)  12 us
    pallas_call x2, Pallas kernels, packed_rows(): pl.pallas_call(patch_kernel, out_shape=jax.ShapeDtypeStruct(shape, jnp.bf...  11.6 us
    all_to_all x1, starting transfers between devices, shards(): arrived0 = lax.all_to_all(packed0, ('z', 'core'), 0, 0, tiled=True)  9.98 us
    all_gather x1, waiting for transfers between devices, shards(): weight = lax.all_gather(embed_weight, 'fsdp', axis=0, tiled=True)  9.82 us
  transfers between devices with their start and end apart: 10, of which 9 were waited for; matrix products, arithmetic and copies ran while one was open for 2% of the time, Pallas kernels for 10%

profile of v2, /device:TPU:1, one launch (start us, length us, event | category | flops | bytes accessed | tf_op | source)
XLA Modules:
  0.0 203.3 jit_solution(5422819345048076823)
XLA Ops:
  7.2 5.8 %patch_rows.3 = bf16[16,296,128]{2,1,0:T(8,128)(2,1)} custom-call(s32[1]{0:T(128)} %constant.20.clone.1.valid_ref, s32[1,512]{1,0:T(1,128)} %bitcast.17, bf16[1,1,4,3,224,224]{5,4,3,2,1,0:T(8,128)(2,1)} %fb_ref.3, bf16[1,1,4,3,224,224]{5,4,3,2,1,0:T(8,128)(2,1)} %fb_ref.3), custom_call_target="tpu_custom_call" | custom-call | tf_op jit(solution)/shard_map/patch_rows/pallas_call | solution.py:127
  13.0 10.0 %all-to-all-start.1 = ((bf16[16,296,128]{2,1,0:T(8,128)(2,1)}), bf16[16,296,128]{2,1,0:T(8,128)(2,1)S(1)}, u32[]{:S(2)}, u32[]{:S(2)}) async-start(bf16[16,296,128]{2,1,0:T(8,128)(2,1)} %patch_rows.3), calls=%async_computation.1 | async-start | bytes 2424832 | tf_op jit(solution)/shard_map/all_to_all | solution.py:434
  26.0 9.6 %collective-permute-done.fa_ref = bf16[1,1,1,3,224,224]{5,4,3,2,1,0:T(8,128)(2,1)S(1)} collective-permute-done((bf16[1,1,1,3,224,224]{5,4,3,2,1,0:T(8,128)(2,1)S(1)}, bf16[1,1,1,3,224,224]{5,4,3,2,1,0:T(8,128)(2,1)S(1)}, u32[]{:S(2)}, u32[]{:S(2)}) %collective-permute-start) | collective-permute-done | bytes 301088 | tf_op jit(solution)/shard_map/ppermute | solution.py:429
  36.4 5.8 %patch_rows.2 = bf16[16,296,128]{2,1,0:T(8,128)(2,1)} custom-call(s32[1]{0:T(128)} %bitcast.3.valid_ref, s32[1,512]{1,0:T(1,128)} %bitcast.18, bf16[1,1,1,3,224,224]{5,4,3,2,1,0:T(8,128)(2,1)} %copy-done.7, bf16[1,1,4,3,224,224]{5,4,3,2,1,0:T(8,128)(2,1)} %fb_ref.3), custom_call_target="tpu_custom_call" | custom-call | tf_op jit(solution)/shard_map/patch_rows/pallas_call | solution.py:127
  42.2 12.0 %all-to-all-done.1.arr_ref = bf16[16,296,128]{2,1,0:T(8,128)(2,1)S(1)} async-done(((bf16[16,296,128]{2,1,0:T(8,128)(2,1)}), bf16[16,296,128]{2,1,0:T(8,128)(2,1)S(1)}, u32[]{:S(2)}, u32[]{:S(2)}) %all-to-all-start.1) | async-done | bytes 1212448 | tf_op jit(solution)/shard_map/all_to_all | solution.py:434
  54.2 3.7 %all-to-all-start = ((bf16[16,296,128]{2,1,0:T(8,128)(2,1)}), bf16[16,296,128]{2,1,0:T(8,128)(2,1)S(1)}, u32[]{:S(2)}, u32[]{:S(2)}) async-start(bf16[16,296,128]{2,1,0:T(8,128)(2,1)} %patch_rows.2), calls=%async_computation | async-start | bytes 2424832 | tf_op jit(solution)/shard_map/all_to_all | solution.py:436
  60.1 9.8 %all-gather.2.cloned.1.call-done.w_ref = bf16[1280,1176]{1,0:T(8,128)(2,1)} async-done(((bf16[320,1176]{1,0:T(8,128)(2,1)}), bf16[1280,1176]{1,0:T(8,128)(2,1)}) %all-gather.2.cloned.1.call-update) | async-done | bytes 3010576 | tf_op jit(solution)/shard_map/all_gather | solution.py:430
  69.9 8.1 %weight_columns.1.w_ref = bf16[1280,1280]{1,0:T(8,128)(2,1)} custom-call(s32[1,1176]{1,0:T(1,128)} %constant.22.clone.place_ref, bf16[1280,1176]{1,0:T(8,128)(2,1)} %all-gather.2.cloned.1.call-done.w_ref), custom_call_target="tpu_custom_call" | custom-call | tf_op jit(solution)/shard_map/weight_columns/pallas_call | solution.py:156
  78.0 6.5 %first_half.1 = (bf16[512,640]{1,0:T(8,128)(2,1)}, f32[512,1280]{1,0:T(8,128)}) custom-call(s32[512,1]{1,0:T(8,128)} %copy.13.slot_ref, bf16[16,296,128]{2,1,0:T(8,128)(2,1)} %copy-done.1, bf16[1280,1280]{1,0:T(8,128)(2,1)} %weight_columns.1.w_ref), custom_call_target="tpu_custom_call" | custom-call | tf_op jit(solution)/shard_map/first_half/pallas_call | solution.py:198
  84.5 4.7 %all-to-all-done.arr_ref = bf16[16,296,128]{2,1,0:T(8,128)(2,1)S(1)} async-done(((bf16[16,296,128]{2,1,0:T(8,128)(2,1)}), bf16[16,296,128]{2,1,0:T(8,128)(2,1)S(1)}, u32[]{:S(2)}, u32[]{:S(2)}) %all-to-all-start) | async-done | bytes 1212448 | tf_op jit(solution)/shard_map/all_to_all | solution.py:436
  90.2 4.5 %second_half.1 = (bf16[512,640]{1,0:T(8,128)(2,1)}, bf16[512,640]{1,0:T(8,128)(2,1)}, bf16[512,640]{1,0:T(8,128)(2,1)}) custom-call(s32[2]{0:T(128)} %pad_add_fusion.core_ref, s32[512,1]{1,0:T(8,128)} %copy.13.slot_ref, bf16[16,296,128]{2,1,0:T(8,128)(2,1)} %copy-done, bf16[512,640]{1,0:T(8,128)(2,1)} %get-tuple-element.11.rows0_ref), custom_call_target="tpu_custom_call" | custom-call | tf_op jit(solution)/shard_map/second_half/pallas_call | solution.py:234
  94.7 14.0 %norm_backward.1 = (bf16[512,1280]{1,0:T(8,128)(2,1)}, f32[16,1280]{1,0:T(8,128)}) custom-call(bf16[512,640]{1,0:T(8,128)(2,1)} %get-tuple-element.12.rows_ref, f32[512,1280]{1,0:T(8,128)} %get-tuple-element.13.part_ref, bf16[1280,1280]{1,0:T(8,128)(2,1)} %weight_columns.1.w_ref, bf16[1,1,512,1280]{3,2,1,0:T(8,128)(2,1)} %g_ref.1, ...), custom_call_target="tpu_custom_call" | custom-call | tf_op jit(solution)/shard_map/norm_backward/pallas_call | solution.py:278
  109.2 3.5 %collective-permute-done.2.rows1_ref = bf16[512,640]{1,0:T(8,128)(2,1)S(1)} collective-permute-done((bf16[512,640]{1,0:T(8,128)(2,1)S(1)}, bf16[512,640]{1,0:T(8,128)(2,1)S(1)}, u32[]{:S(2)}, u32[]{:S(2)}) %collective-permute-start.2) | collective-permute-done | bytes 655392 | tf_op jit(solution)/shard_map/ppermute | solution.py:441
  113.9 6.6 %products.1 = (f32[1600,128]{1,0:T(8,128)}, bf16[3,1600,128]{2,1,0:T(8,128)(2,1)}) custom-call(s32[2]{0:T(128)} %pad_add_fusion.core_ref, bf16[512,1280]{1,0:T(8,128)(2,1)} %get-tuple-element.14.grad0_ref, bf16[512,1280]{1,0:T(8,128)(2,1)} %copy-done.3, bf16[512,640]{1,0:T(8,128)(2,1)} %get-tuple-element.15.rows0_ref, bf16[512,640]{1,0:T(8,128)(2,1)} %copy-done.6, ...), custom_call_target="tpu_custom_call" | custom-call | tf_op jit(solution)/shard_map/products/pallas_call | solution.py:332
  124.7 1.5 collective-permute-start.5
  126.2 4.1 %collective-permute-done.3 = bf16[1600,128]{1,0:T(8,128)(2,1)S(1)} collective-permute-done((bf16[1600,128]{1,0:T(8,128)(2,1)S(1)}, bf16[1600,128]{1,0:T(8,128)(2,1)S(1)}, u32[]{:S(2)}, u32[]{:S(2)}) %collective-permute-start.3) | collective-permute-done | bytes 409632 | tf_op jit(solution)/shard_map/ppermute | solution.py:445
  130.3 5.4 %collective-permute-done.5 = bf16[1600,128]{1,0:T(8,128)(2,1)S(1)} collective-permute-done((bf16[1600,128]{1,0:T(8,128)(2,1)S(1)}, bf16[1600,128]{1,0:T(8,128)(2,1)S(1)}, u32[]{:S(2)}, u32[]{:S(2)}) %collective-permute-start.5) | collective-permute-done | bytes 409632 | tf_op jit(solution)/shard_map/ppermute | solution.py:445
  135.9 12.3 %all_to_all.30 = f32[4,400,128]{2,1,0:T(8,128)S(1)} all-to-all(f32[4,400,128]{2,1,0:T(8,128)S(1)} %bitcast.14), channel_id=1, replica_groups={{0,4,8,12},{1,5,9,13},{2,6,10,14},{3,7,11,15},{16,17,18,19},{20,21,22,2..., dimensions={0} | all-to-all | bytes 1638400 | tf_op jit(solution)/shard_map/all_to_all | solution.py:449
  148.3 12.1 %all_to_all.31 = f32[8,56,128]{2,1,0:T(8,128)S(1)} all-to-all(f32[8,56,128]{2,1,0:T(8,128)S(1)} %bitcast.15), channel_id=1, replica_groups=mesh['z'=8,'core'=2,'slab'=4,'fsdp'=4] {'z'}, dimensions={0} | all-to-all | bytes 458752 | tf_op jit(solution)/shard_map/all_to_all | solution.py:453
  160.4 11.4 %all_to_all.32 = f32[8,56,128]{2,1,0:T(8,128)S(1)} all-to-all(f32[8,56,128]{2,1,0:T(8,128)S(1)} %broadcast_in_dim.20), channel_id=1, replica_groups=mesh['z'=8,'core'=2,'slab'=4,'fsdp'=4] {'z'}, dimensions={0} | all-to-all | bytes 458752 | tf_op jit(solution)/shard_map/all_to_all | solution.py:420
  171.8 12.0 %all_to_all.33.mine_ref = f32[4,448,128]{2,1,0:T(8,128)S(1)} all-to-all(f32[4,448,128]{2,1,0:T(8,128)S(1)} %broadcast_in_dim.22), channel_id=1, replica_groups=mesh['z'=8,'core'=2,'slab'=4,'fsdp'=4] {'slab'}, dimensions={0} | all-to-all | bytes 1835008 | tf_op jit(solution)/shard_map/all_to_all | solution.py:420
  183.8 5.9 %collective-permute-start.6 = (f32[4,448,128]{2,1,0:T(8,128)S(1)}, f32[4,448,128]{2,1,0:T(8,128)S(1)}, u32[]{:S(2)}, u32[]{:S(2)}) collective-permute-start(f32[4,448,128]{2,1,0:T(8,128)S(1)} %all_to_all.33.mine_ref), channel_id=1, source_target_pairs={{0,16},{16,0},{1,17},{17,1},{2,18},{18,2},{3,19},{19,3},{4,20},{20... | collective-permute-start | bytes 2752520 | tf_op jit(solution)/shard_map/ppermute | solution.py:456
  189.7 2.1 %collective-permute-done.6.other_ref = f32[4,448,128]{2,1,0:T(8,128)S(1)} collective-permute-done((f32[4,448,128]{2,1,0:T(8,128)S(1)}, f32[4,448,128]{2,1,0:T(8,128)S(1)}, u32[]{:S(2)}, u32[]{:S(2)}) %collective-permute-start.6) | collective-permute-done | bytes 917536 | tf_op jit(solution)/shard_map/ppermute | solution.py:456
  192.8 3.6 %column_order.1 = (f32[320,1176]{1,0:T(8,128)}, f32[2,320]{1,0:T(2,128)}) custom-call(s32[2]{0:T(128)} %pad_add_fusion.core_ref, f32[4,448,128]{2,1,0:T(8,128)} %copy-done.2, f32[4,448,128]{2,1,0:T(8,128)} %copy-done.4), custom_call_target="tpu_custom_call" | custom-call | tf_op jit(solution)/shard_map/column_order/pallas_call | solution.py:388
  (42 shorter events, 14.1 us)
Async XLA Ops:
  13.0 41.2 %all-to-all-start.1 = ((bf16[16,296,128]{2,1,0:T(8,128)(2,1)}), bf16[16,296,128]{2,1,0:T(8,128)(2,1)S(1)}, u32[]{:S(2)}, u32[]{:S(2)}) async-start(bf16[16,296,128]{2,1,0:T(8,128)(2,1)} %patch_rows.3), calls=%async_computation.1 | async-start | bytes 2424832 | tf_op jit(solution)/shard_map/all_to_all | solution.py:434
  23.0 46.9 %all-gather.2.cloned.1.call-start = ((), (), s32[]{:S(2)}) async-start(), calls=%async_computation.6 | async-start | bytes 4096000 | tf_op jit(solution)/shard_map/all_gather | solution.py:430
  24.7 10.9 %collective-permute-start = (bf16[1,1,1,3,224,224]{5,4,3,2,1,0:T(8,128)(2,1)S(1)}, bf16[1,1,1,3,224,224]{5,4,3,2,1,0:T(8,128)(2,1)S(1)}, u32[]{:S(2)}, u32[]{:S(2)}) collective-permute-start(bf16[1,1,1,3,224,224]{5,4,3,2,1,0:T(8,128)(2,1)S(1)} %slice.12), channel_id=1, source_target_pairs={{0,4},{4,8},{8,12},{12,0},{1,5},{5,9},{9,13},{13,1},{2,6},{6,10},{... | collective-permute-start | bytes 903176 | tf_op jit(solution)/shard_map/ppermute | solution.py:429
  35.6 0.7 copy-start.7
  42.2 15.8 %copy-start.9 = (s32[1,1,512]{2,1,0:T(1,128)S(1)}, s32[1,1,512]{2,1,0:T(1,128)}, u32[]{:S(2)}) copy-start(s32[1,1,512]{2,1,0:T(1,128)} %param.13) | copy-start | bytes 6148
  42.2 16.7 %copy-start.8 = (f32[1280]{0:T(1024)S(1)}, f32[1280]{0:T(1024)}, u32[]{:S(2)}) copy-start(f32[1280]{0:T(1024)} %param.12) | copy-start | bytes 15364
  54.2 4.6 %copy-start.1 = (bf16[16,296,128]{2,1,0:T(8,128)(2,1)}, bf16[16,296,128]{2,1,0:T(8,128)(2,1)S(1)}, u32[]{:S(2)}) copy-start(bf16[16,296,128]{2,1,0:T(8,128)(2,1)S(1)} %all-to-all-done.1.arr_ref) | copy-start | bytes 3637252
  54.2 35.0 %all-to-all-start = ((bf16[16,296,128]{2,1,0:T(8,128)(2,1)}), bf16[16,296,128]{2,1,0:T(8,128)(2,1)S(1)}, u32[]{:S(2)}, u32[]{:S(2)}) async-start(bf16[16,296,128]{2,1,0:T(8,128)(2,1)} %patch_rows.2), calls=%async_computation | async-start | bytes 2424832 | tf_op jit(solution)/shard_map/all_to_all | solution.py:436
  89.2 1.0 copy-start
  94.7 14.0 %copy-start.10 = (bf16[512,640]{1,0:T(8,128)(2,1)S(1)}, bf16[512,640]{1,0:T(8,128)(2,1)}, u32[]{:S(2)}) copy-start(bf16[512,640]{1,0:T(8,128)(2,1)} %get-tuple-element.16) | copy-start | bytes 1966084
  108.7 4.1 %collective-permute-start.1 = (bf16[512,1280]{1,0:T(8,128)(2,1)}, bf16[512,1280]{1,0:T(8,128)(2,1)S(1)}, u32[]{:S(2)}, u32[]{:S(2)}) collective-permute-start(bf16[512,1280]{1,0:T(8,128)(2,1)} %get-tuple-element.14.grad0_ref), channel_id=1, source_target_pairs={{0,16},{16,0},{1,17},{17,1},{2,18},{18,2},{3,19},{19,3},{4,20},{20... | collective-permute-start | bytes 3932168 | tf_op jit(solution)/shard_map/ppermute | solution.py:443
  108.7 4.0 %collective-permute-start.2 = (bf16[512,640]{1,0:T(8,128)(2,1)S(1)}, bf16[512,640]{1,0:T(8,128)(2,1)S(1)}, u32[]{:S(2)}, u32[]{:S(2)}) collective-permute-start(bf16[512,640]{1,0:T(8,128)(2,1)S(1)} %copy-done.10), channel_id=1, source_target_pairs={{0,16},{16,0},{1,17},{17,1},{2,18},{18,2},{3,19},{19,3},{4,20},{20... | collective-permute-start | bytes 1966088 | tf_op jit(solution)/shard_map/ppermute | solution.py:441
  112.6 0.8 copy-start.6
  112.7 1.2 copy-start.3
  120.5 15.2 %copy-start.5 = (f32[1600,128]{1,0:T(8,128)S(1)}, f32[1600,128]{1,0:T(8,128)}, u32[]{:S(2)}) copy-start(f32[1600,128]{1,0:T(8,128)} %get-tuple-element.18) | copy-start | bytes 2457604
  121.9 8.4 %collective-permute-start.3 = (bf16[1600,128]{1,0:T(8,128)(2,1)S(1)}, bf16[1600,128]{1,0:T(8,128)(2,1)S(1)}, u32[]{:S(2)}, u32[]{:S(2)}) collective-permute-start(bf16[1600,128]{1,0:T(8,128)(2,1)S(1)} %get-tuple-element.20), channel_id=1, source_target_pairs={{0,1},{16,20},{1,2},{17,21},{2,3},{18,22},{3,0},{19,23},{4,5},{20,... | collective-permute-start | bytes 1228808 | tf_op jit(solution)/shard_map/ppermute | solution.py:445
  123.2 7.1 %collective-permute-start.4 = (bf16[1600,128]{1,0:T(8,128)(2,1)S(1)}, bf16[1600,128]{1,0:T(8,128)(2,1)S(1)}, u32[]{:S(2)}, u32[]{:S(2)}) collective-permute-start(bf16[1600,128]{1,0:T(8,128)(2,1)S(1)} %get-tuple-element.22), channel_id=1, source_target_pairs={{0,3},{16,28},{1,0},{17,29},{2,1},{18,30},{3,2},{19,31},{4,7},{20,... | collective-permute-start | bytes 1228808 | tf_op jit(solution)/shard_map/ppermute | solution.py:445
  124.7 11.0 %collective-permute-start.5 = (bf16[1600,128]{1,0:T(8,128)(2,1)S(1)}, bf16[1600,128]{1,0:T(8,128)(2,1)S(1)}, u32[]{:S(2)}, u32[]{:S(2)}) collective-permute-start(bf16[1600,128]{1,0:T(8,128)(2,1)S(1)} %get-tuple-element.21), channel_id=1, source_target_pairs={{0,2},{16,24},{1,3},{17,25},{2,0},{18,26},{3,1},{19,27},{4,6},{20,... | collective-permute-start | bytes 1228808 | tf_op jit(solution)/shard_map/ppermute | solution.py:445
  183.8 8.0 %copy-start.2 = (f32[4,448,128]{2,1,0:T(8,128)}, f32[4,448,128]{2,1,0:T(8,128)S(1)}, u32[]{:S(2)}) copy-start(f32[4,448,128]{2,1,0:T(8,128)S(1)} %all_to_all.33.mine_ref) | copy-start | bytes 2752516
  183.8 8.0 %collective-permute-start.6 = (f32[4,448,128]{2,1,0:T(8,128)S(1)}, f32[4,448,128]{2,1,0:T(8,128)S(1)}, u32[]{:S(2)}, u32[]{:S(2)}) collective-permute-start(f32[4,448,128]{2,1,0:T(8,128)S(1)} %all_to_all.33.mine_ref), channel_id=1, source_target_pairs={{0,16},{16,0},{1,17},{17,1},{2,18},{18,2},{3,19},{19,3},{4,20},{20... | collective-permute-start | bytes 2752520 | tf_op jit(solution)/shard_map/ppermute | solution.py:456
  191.8 1.0 copy-start.4
Sparse Core Ops, SparseCore 0:
  25.6 44.2 all-gather.1

commit v3 on v2

v3 whole, which is shorter than its diff:
```python
import jax
import jax.numpy as jnp
import numpy as np
from jax import lax
from jax.experimental import pallas as pl
from jax.experimental.pallas import tpu as pltpu
from jax.sharding import Mesh
from jax.sharding import PartitionSpec as P

GH = 16
GW = 16
PS = 14
COLOURS = 3
SIDE = 224
ROWS = 512
CAP = 64
PEERS = 16
D = 1280
KIN = 1176
GROUPS = 9
PARTS = COLOURS * PS
FRAME = PARTS * PS
HELD = 296
HALF = 640
TILES = HALF // 128
OWNED = D // 4
LINE = OWNED * TILES
QUARTER = LINE // 4
STEP = 80
PIECE = 56
BLOCK = 128
SUMS = 96
VMEM = 60 * 1024 * 1024
ALL = pl.BlockSpec(memory_space=pltpu.VMEM)
SCALAR = pl.BlockSpec(memory_space=pltpu.SMEM)
PARAMS = pltpu.CompilerParams(vmem_limit_bytes=VMEM)
LANES = (((1,), (1,)), ((), ()))
SUBLANES = (((0,), (0,)), ((), ()))


def one_hot(match):
    return match.astype(jnp.float32).astype(jnp.bfloat16)


def iota(shape, dim):
    return lax.broadcasted_iota(jnp.int32, shape, dim)


def dot(a, b, dims=(((1,), (0,)), ((), ()))):
    return lax.dot_general(a, b, dims, preferred_element_type=jnp.float32)


def column_places():
    place = np.zeros((1, KIN), np.int32)
    for c in range(COLOURS):
        for t in range(2):
            part = c * PS * PS + np.arange(PS * PS)
            at = (c * 2 + t) * PS * PS
            place[0, at : at + PS * PS] = (1 - t) * HALF + part
    return place


def patch_kernel(valid_ref, slot_ref, fa_ref, fb_ref, out_ref, spread_ref, rows_ref):
    src = iota((SIDE, 256), 0)
    place = jnp.where(src >= GROUPS * PS, src + 2, src)
    spread = one_hot(iota((SIDE, 256), 1) == place)
    for k, ref in enumerate((fa_ref, fb_ref)):
        for c in range(COLOURS):
            wide = dot(ref[0, 0, 0, c], spread)
            for h in range(2):
                spread_ref[k, c, h] = wide[:, h * 128 : (h + 1) * 128]

    @pl.when(valid_ref[0] == 0)
    def _():
        spread_ref[0] = jnp.zeros_like(spread_ref[0])

    lane = iota((GH, 128), 1)
    for k in range(2):
        for x in range(GW):
            here = slice((k * GW + x) * GH, (k * GW + x + 1) * GH)
            acc = None
            for n in range(PARTS):
                c, p = divmod(n, PS)
                piece = spread_ref[k, c, x // GROUPS, pl.ds(p, GH, stride=PS), :]
                shift = PS * (n - x % GROUPS) % 128
                if shift:
                    piece = pltpu.roll(piece, shift, 1)
                tile, at = divmod(PS * n, 128)
                acc = piece if acc is None else jnp.where(lane >= at, piece, acc)
                if n == PARTS - 1:
                    acc = jnp.where(lane < at + PS, acc, 0.0)
                if at + PS >= 128 or n == PARTS - 1:
                    rows_ref[here, tile * 128 : (tile + 1) * 128] = acc.astype(jnp.bfloat16)
                    acc = piece
    slots = slot_ref[...]
    kind = iota((16, ROWS), 0)
    digits = jnp.where(kind == 0, slots >> 6, jnp.where(kind == 1, slots & 63, 0))
    dst = iota((ROWS, ROWS), 0)
    order = one_hot(iota((ROWS, ROWS), 1) == (dst & 256) + ((dst & 15) << 4) + ((dst >> 4) & 15))
    digits = dot(order, digits.astype(jnp.float32).astype(jnp.bfloat16), LANES)
    slots = (digits[:, 0:1] * 64.0 + digits[:, 1:2]).astype(jnp.int32)
    side = iota((HELD, 128), 1) < CAP
    for i in range(PEERS // 4):
        pick = one_hot(iota((ROWS, 256), 1) + i * 256 == slots)
        both = dot(rows_ref[...], pick, SUBLANES)
        for j in range(2):
            lo = both[0:HELD, j * 128 : (j + 1) * 128]
            hi = both[HELD : 2 * HELD, j * 128 : (j + 1) * 128]
            peer = i * 4 + j * 2
            out_ref[peer] = jnp.where(side, lo, pltpu.roll(hi, CAP, 1)).astype(jnp.bfloat16)
            out_ref[peer + 1] = jnp.where(side, pltpu.roll(lo, CAP, 1), hi).astype(jnp.bfloat16)


def packed_rows(valid, slots, first, second, first_at, second_at):
    block = (1, 1, 1, COLOURS, SIDE, SIDE)
    shape = (PEERS, HELD, 128)
    return pl.pallas_call(
        patch_kernel,
        out_shape=jax.ShapeDtypeStruct(shape, jnp.bfloat16),
        grid=(1,),
        in_specs=[
            SCALAR,
            pl.BlockSpec((1, ROWS), lambda i: (0, 0)),
            pl.BlockSpec(block, lambda i: (0, 0, first_at, 0, 0, 0)),
            pl.BlockSpec(block, lambda i: (0, 0, second_at, 0, 0, 0)),
        ],
        out_specs=pl.BlockSpec(shape, lambda i: (0, 0, 0)),
        scratch_shapes=[
            pltpu.VMEM((2, COLOURS, 2, SIDE, 128), jnp.float32),
            pltpu.VMEM((ROWS, HALF), jnp.bfloat16),
        ],
        compiler_params=PARAMS,
        name="patch_rows",
    )(valid, slots, first, second)


def weight_kernel(place_ref, w_ref, out_ref):
    for i in range(2):
        pick = one_hot(iota((HALF, KIN), 0) + i * HALF == place_ref[...])
        out_ref[:, i * HALF : (i + 1) * HALF] = dot(w_ref[...], pick, LANES).astype(jnp.bfloat16)


def padded_weight(weight):
    return pl.pallas_call(
        weight_kernel,
        out_shape=jax.ShapeDtypeStruct((weight.shape[0], 2 * HALF), jnp.bfloat16),
        compiler_params=PARAMS,
        name="weight_columns",
    )(jnp.asarray(column_places()), weight)


def taken_rows(slot_ref, arr_ref, cols_ref):
    side = iota((HELD, 128), 1) < CAP
    for j in range(PEERS // 2):
        even = arr_ref[2 * j].astype(jnp.float32)
        odd = arr_ref[2 * j + 1].astype(jnp.float32)
        low = jnp.where(side, even, pltpu.roll(odd, CAP, 1))
        high = jnp.where(side, pltpu.roll(even, CAP, 1), odd)
        both = jnp.concatenate([low, high], axis=0).astype(jnp.bfloat16)
        cols_ref[: 2 * HELD, j * 128 : (j + 1) * 128] = both
    cols_ref[2 * HELD :, :] = jnp.zeros((HALF - 2 * HELD, PEERS * CAP), jnp.bfloat16)
    pick = one_hot(iota((ROWS, PEERS * CAP), 1) == slot_ref[...])
    return dot(pick, cols_ref[...], LANES).astype(jnp.bfloat16)


def first_kernel(slot_ref, arr_ref, w_ref, rows_ref, part_ref, cols_ref):
    rows_ref[...] = taken_rows(slot_ref, arr_ref, cols_ref)
    for i in range(ROWS // 128):
        here = slice(i * 128, (i + 1) * 128)
        part_ref[here, :] = dot(rows_ref[here, :], w_ref[:, :HALF], LANES)


def first_half(slots, arrived, weight):
    return pl.pallas_call(
        first_kernel,
        out_shape=(
            jax.ShapeDtypeStruct((ROWS, HALF), jnp.bfloat16),
            jax.ShapeDtypeStruct((ROWS, D), jnp.float32),
        ),
        in_specs=[ALL] * 3,
        out_specs=(ALL, ALL),
        scratch_shapes=[pltpu.VMEM((HALF, PEERS * CAP), jnp.bfloat16)],
        compiler_params=PARAMS,
        name="first_half",
    )(slots, arrived, weight)


def backward_kernel(core_ref, slot_ref, arr_ref, rows0_ref, part_ref, w_ref, g_ref, r_ref, gain_ref, grad_ref, mine_ref, send_ref, sums_ref, cols_ref, rows1_ref):
    rows1_ref[...] = taken_rows(slot_ref, arr_ref, cols_ref)

    @pl.when(core_ref[0] == 0)
    def _():
        mine_ref[...] = rows0_ref[...]
        send_ref[...] = rows1_ref[...]

    @pl.when(core_ref[0] != 0)
    def _():
        mine_ref[...] = rows1_ref[...]
        send_ref[...] = rows0_ref[...]

    gain = gain_ref[...]
    gain_sums = jnp.zeros((8, D), jnp.float32)
    bias_sums = jnp.zeros((8, D), jnp.float32)
    for i in range(ROWS // BLOCK):
        here = slice(i * BLOCK, (i + 1) * BLOCK)
        embedded = part_ref[here, :] + dot(rows1_ref[here, :], w_ref[:, HALF:], LANES)
        deviation = embedded - jnp.mean(embedded, axis=-1, keepdims=True)
        variance = jnp.mean(deviation * deviation, axis=-1, keepdims=True)
        inverse_std = lax.rsqrt(variance + 1e-06)
        normalized = deviation * inverse_std
        upstream_norm = g_ref[0, 0, here, :].astype(jnp.float32)
        upstream = upstream_norm * gain
        inner = jnp.mean(upstream * normalized, axis=-1, keepdims=True)
        level = jnp.mean(upstream, axis=-1, keepdims=True)
        input_grad = r_ref[0, 0, here, :].astype(jnp.float32) + inverse_std * (
            upstream - level - normalized * inner
        )
        grad_ref[here, :] = input_grad.astype(jnp.bfloat16)
        gain_sums += jnp.sum((upstream_norm * normalized).reshape(BLOCK // 8, 8, D), axis=0)
        bias_sums += jnp.sum(upstream_norm.reshape(BLOCK // 8, 8, D), axis=0)
    sums_ref[0:8, :] = gain_sums
    sums_ref[8:16, :] = bias_sums


def norm_backward(core, slots, arrived, rows0, part, weight, grad_norm, grad_resid, gain):
    half = jax.ShapeDtypeStruct((ROWS, HALF), jnp.bfloat16)
    return pl.pallas_call(
        backward_kernel,
        out_shape=(
            jax.ShapeDtypeStruct((ROWS, D), jnp.bfloat16),
            half,
            half,
            jax.ShapeDtypeStruct((16, D), jnp.float32),
        ),
        in_specs=[SCALAR] + [ALL] * 8,
        out_specs=(ALL,) * 4,
        scratch_shapes=[
            pltpu.VMEM((HALF, PEERS * CAP), jnp.bfloat16),
            pltpu.VMEM((ROWS, HALF), jnp.bfloat16),
        ],
        compiler_params=PARAMS,
        name="norm_backward",
    )(core, slots, arrived, rows0, part, weight, grad_norm, grad_resid, gain)


def product_kernel(core_ref, grad0_ref, grad1_ref, rows0_ref, rows1_ref, sums_ref, own_ref, out1_ref, out2_ref, out3_ref, terms_ref):
    core, place = core_ref[0], core_ref[1]
    kind = iota((128, HALF), 0)
    for i in range(D // HALF):
        here = slice(i * HALF, (i + 1) * HALF)
        terms_ref[...] = dot(grad0_ref[:, here], rows0_ref[...], SUBLANES) + dot(
            grad1_ref[:, here], rows1_ref[...], SUBLANES
        )
        gain_sum = jnp.sum(sums_ref[0:8, here], axis=0, keepdims=True)
        bias_sum = jnp.sum(sums_ref[8:16, here], axis=0, keepdims=True)
        sums = jnp.where(kind == SUMS, gain_sum, jnp.where(kind == SUMS + 1, bias_sum, 0.0))
        terms_ref[:, HALF - 128 :] += sums.T
        for n in range(HALF // STEP):
            y, r = divmod(i * (HALF // STEP) + n, OWNED // STEP)
            for t in range(TILES):
                o = t * (OWNED // STEP) + r
                block = terms_ref[n * STEP : (n + 1) * STEP, t * 128 : (t + 1) * 128]
                to = jnp.where(core == 0, y, o // 5)
                at = jnp.where(core == 0, o * STEP, y * QUARTER + o % 5 * STEP)
                at = pl.ds(pl.multiple_of(at, 16), STEP)
                by = (to - place) & 3
                for n_by, ref in enumerate((own_ref, out1_ref, out2_ref, out3_ref)):

                    @pl.when(by == n_by)
                    def _(ref=ref, at=at, block=block):
                        ref[at, :] = block.astype(ref.dtype)


def products(core, grad0, grad1, rows0, rows1, sums):
    sent = jax.ShapeDtypeStruct((LINE, 128), jnp.bfloat16)
    return pl.pallas_call(
        product_kernel,
        out_shape=(jax.ShapeDtypeStruct((LINE, 128), jnp.float32), sent, sent, sent),
        in_specs=[SCALAR] + [ALL] * 5,
        out_specs=(ALL,) * 4,
        scratch_shapes=[pltpu.VMEM((HALF, HALF), jnp.float32)],
        compiler_params=PARAMS,
        name="products",
    )(core, grad0, grad1, rows0, rows1, sums)


def runs():
    place = column_places()[0]
    found = []
    at = 0
    while at < KIN:
        stop = at + 1
        while stop < KIN and place[stop] == place[stop - 1] + 1 and place[stop] % 128 and stop % 128:
            stop += 1
        found.append((at, int(place[at]), stop - at))
        at = stop
    return found


def finish_kernel(core_ref, mine_ref, other_ref, out_ref, norm_ref, held_ref, last_ref):
    core = core_ref[0]
    for t in range(TILES):
        for r in range(OWNED // STEP):
            x, w = divmod(t * (OWNED // STEP) + r, 5)
            source = slice(x * 8 * PIECE + w * STEP, x * 8 * PIECE + (w + 1) * STEP)
            at = slice(r * STEP, (r + 1) * STEP)
            held_ref[core * TILES + t, at, :] = mine_ref[source, :]
            held_ref[(1 - core) * TILES + t, at, :] = other_ref[source, :]
    lane = iota((OWNED, 128), 1)
    for tile in range(pl.cdiv(KIN, 128)):
        acc = None
        for at, src, size in runs():
            if at // 128 != tile:
                continue
            piece = held_ref[src // 128]
            shift = (at - src) % 128
            if shift:
                piece = pltpu.roll(piece, shift, 1)
            acc = piece if acc is None else jnp.where(lane >= at % 128, piece, acc)
        width = min(128, KIN - tile * 128)
        out_ref[:, tile * 128 : tile * 128 + width] = acc[:, :width]
    last_ref[0:OWNED, :] = held_ref[TILES - 1] + held_ref[2 * TILES - 1]
    last_ref[OWNED:, :] = jnp.zeros((384 - OWNED, 128), jnp.float32)
    norm_ref[...] = last_ref[...].T[SUMS : SUMS + 2, :OWNED]


def finish(core, mine, other):
    return pl.pallas_call(
        finish_kernel,
        out_shape=(
            jax.ShapeDtypeStruct((OWNED, KIN), jnp.float32),
            jax.ShapeDtypeStruct((2, OWNED), jnp.float32),
        ),
        in_specs=[SCALAR, ALL, ALL],
        out_specs=(ALL, ALL),
        scratch_shapes=[
            pltpu.VMEM((2 * TILES, OWNED, 128), jnp.float32),
            pltpu.VMEM((384, 128), jnp.float32),
        ],
        compiler_params=PARAMS,
        name="column_order",
    )(core, mine, other)


def plane_index(core, x, y):
    return (core * 4 + x) * 4 + y


def plane_shift(by):
    pairs = []
    for x in range(4):
        for y in range(4):
            pairs.append((plane_index(0, x, y), plane_index(0, x, (y + by) % 4)))
            pairs.append((plane_index(1, x, y), plane_index(1, (x + by) % 4, y)))
    return pairs


def copies(array, axis, count):
    array = jnp.broadcast_to(array[None], (count,) + array.shape)
    return lax.all_to_all(array, axis, 0, 0, tiled=True)


def shards(pixels, grad_norm, grad_resid, embed_weight, norm_gain, send_slot, recv_slot):
    plane = ("core", "slab", "fsdp")
    core = lax.axis_index("core").astype(jnp.int32)
    x = lax.axis_index("slab").astype(jnp.int32)
    y = lax.axis_index("fsdp").astype(jnp.int32)
    place = jnp.stack([core, jnp.where(core == 0, y, x)])
    earlier = lax.ppermute(pixels[:, :, 3:4], "slab", [(i, (i + 1) % 4) for i in range(4)])
    takes = recv_slot.reshape(1, ROWS)
    sends = send_slot.reshape(ROWS, 1)
    packed0 = packed_rows(jnp.ones((1,), jnp.int32), takes, pixels, pixels, 0, 2)
    packed0, embed_weight = lax.optimization_barrier((packed0, embed_weight))
    arrived0 = lax.all_to_all(packed0, ("z", "core"), 0, 0, tiled=True)
    weight = lax.all_gather(padded_weight(embed_weight), "fsdp", axis=0, tiled=True)
    packed1 = packed_rows((x > 0).astype(jnp.int32)[None], takes, earlier, pixels, 0, 1)
    arrived1 = lax.all_to_all(packed1, ("z", "core"), 0, 0, tiled=True)
    rows0, part = first_half(sends, arrived0, weight)
    grads, mine, send, sums = norm_backward(
        place, sends, arrived1, rows0, part, weight, grad_norm, grad_resid, norm_gain.reshape(1, D)
    )
    swap = [(0, 1), (1, 0)]
    theirs = lax.ppermute(send, "core", swap)
    their_grads = lax.ppermute(grads, "core", swap)
    own, *sent = products(place, grads, their_grads, mine, theirs, sums)
    terms = [lax.ppermute(sent[by - 1], plane, plane_shift(by)) for by in (1, 3, 2)]
    line = own + terms[0].astype(jnp.float32) + terms[1].astype(jnp.float32) + terms[2].astype(jnp.float32)
    across = [[plane_index(0, i, j) for i in range(4)] for j in range(4)]
    across += [[plane_index(1, i, j) for j in range(4)] for i in range(4)]
    quarters = lax.all_to_all(
        line.reshape(4, QUARTER, 128), plane, 0, 0, tiled=True, axis_index_groups=across
    )
    quarter = jnp.pad(jnp.sum(quarters, axis=0), ((0, 8 * PIECE - QUARTER), (0, 0)))
    pieces = lax.all_to_all(quarter.reshape(8, PIECE, 128), "z", 0, 0, tiled=True)
    line = copies(jnp.sum(pieces, axis=0), ("slab", "z"), 32).reshape(32 * PIECE, 128)
    return finish(place, line, lax.ppermute(line, "core", swap))


def solution(mesh):
    split = Mesh(mesh.devices.reshape(8, 2, 4, 4), ("z", "core", "slab", "fsdp"))
    dp = ("z", "core")
    return jax.shard_map(
        shards,
        mesh=split,
        in_specs=(
            P(dp, "fsdp", "slab", None, None, None),
            P("slab", "fsdp", dp, None),
            P("slab", "fsdp", dp, None),
            P("fsdp", None),
            P(),
            P("slab", "fsdp", dp),
            P("slab", "fsdp", dp),
        ),
        out_specs=(P("fsdp", None), P(None, "fsdp")),
        check_vma=False,
    )
```

time: 204 us -> 201 us (0.985)
  Pallas kernels: 55 us -> 43.3 us
  waiting for transfers between devices: 51.9 us -> 59.8 us
  starting transfers between devices: 25.8 us -> 28 us
    all_to_all x1, waiting for transfers between devices: 4.65 us -> 21.5 us  [shards(): arrived1 = lax.all_to_all(packed1, ('z', 'core'), 0, 0, tiled=True)]
    pallas_call x3 -> x2, Pallas kernels: 26.6 us -> 14.2 us  [the longest x1 10.7 us: norm_backward(): pl.pallas_call(backward_kernel, out_shape=(jax.ShapeDtypeStruct((ROWS, D)...]
    all_gather x1, waiting for transfers between devices: 9.82 us -> 0.09 us  [shards(): lax.all_gather(padded_weight(embed_weight), 'fsdp', axis=0, tiled=True)]
    ppermute x1, starting transfers between devices: 5.9 us -> 8.16 us  [shards(): return finish(place, line, lax.ppermute(line, 'core', swap))]
    all_to_all x2 -> x1, blocking collectives: 23.3 us -> 21.8 us  [copies(): return lax.all_to_all(array, axis, 0, 0, tiled=True)]
  transfers between devices with their start and end apart: 10 -> 10, of which waited for: 9 -> 9; matrix products, arithmetic and copies ran while one was open for 2% -> 2% of each run, Pallas kernels for 10% -> 6%
where the time goes in v3:
time: 201 us; the launch traced here: 200 us
  waiting for transfers between devices  59.8 us (30%)
  blocking collectives  46.2 us (23%)
  Pallas kernels  43.3 us (22%)
  starting transfers between devices  28 us (14%)
  between operations  14.1 us (7%)
  local copies, waits for them, and re-layouts  6.59 us (3%)
    all_to_all x1, blocking collectives, copies(): return lax.all_to_all(array, axis, 0, 0, tiled=True)  21.8 us
    all_to_all x1, waiting for transfers between devices, shards(): arrived1 = lax.all_to_all(packed1, ('z', 'core'), 0, 0, tiled=True)  21.5 us
    all_to_all x1, waiting for transfers between devices, shards(): arrived0 = lax.all_to_all(packed0, ('z', 'core'), 0, 0, tiled=True)  13.1 us
    all_to_all x1, blocking collectives, shards(): lax.all_to_all(line.reshape(4, QUARTER, 128), plane, 0, 0, tiled=True, ax...  12.3 us
    all_to_all x1, blocking collectives, shards(): lax.all_to_all(quarter.reshape(8, PIECE, 128), 'z', 0, 0, tiled=True)  12.1 us
    pallas_call x1, Pallas kernels, norm_backward(): pl.pallas_call(backward_kernel, out_shape=(jax.ShapeDtypeStruct((ROWS, D)...  10.7 us
    pallas_call x2, Pallas kernels, packed_rows(): pl.pallas_call(patch_kernel, out_shape=jax.ShapeDtypeStruct(shape, jnp.bf...  10.7 us
    all_to_all x1, starting transfers between devices, shards(): arrived0 = lax.all_to_all(packed0, ('z', 'core'), 0, 0, tiled=True)  9.99 us
  transfers between devices with their start and end apart: 10, of which 9 were waited for; matrix products, arithmetic and copies ran while one was open for 2% of the time, Pallas kernels for 6%

profile of v3, /device:TPU:1, one launch (start us, length us, event | category | flops | bytes accessed | tf_op | source)
XLA Modules:
  0.0 200.0 jit_solution(6894123292316375469)
XLA Ops:
  7.2 5.3 %patch_rows.3 = bf16[16,296,128]{2,1,0:T(8,128)(2,1)} custom-call(s32[1]{0:T(128)} %constant.20.clone.1.valid_ref, s32[1,512]{1,0:T(1,128)} %bitcast.12, bf16[1,1,4,3,224,224]{5,4,3,2,1,0:T(8,128)(2,1)} %fb_ref.3, bf16[1,1,4,3,224,224]{5,4,3,2,1,0:T(8,128)(2,1)} %fb_ref.3), custom_call_target="tpu_custom_call" | custom-call | tf_op jit(solution)/shard_map/patch_rows/pallas_call | solution.py:117
  12.5 3.6 %weight_columns.1 = bf16[320,1280]{1,0:T(8,128)(2,1)} custom-call(s32[1,1176]{1,0:T(1,128)} %constant.22.clone.place_ref, bf16[320,1176]{1,0:T(8,128)(2,1)} %w_ref), custom_call_target="tpu_custom_call" | custom-call | tf_op jit(solution)/shard_map/weight_columns/pallas_call | solution.py:144
  16.1 10.0 %all-to-all-start.1 = ((bf16[16,296,128]{2,1,0:T(8,128)(2,1)}), bf16[16,296,128]{2,1,0:T(8,128)(2,1)S(1)}, u32[]{:S(2)}, u32[]{:S(2)}) async-start(bf16[16,296,128]{2,1,0:T(8,128)(2,1)} %patch_rows.3), calls=%async_computation.1 | async-start | bytes 2424832 | tf_op jit(solution)/shard_map/all_to_all | solution.py:374
  27.1 1.3 collective-permute-start
  28.4 9.7 %collective-permute-done.fa_ref = bf16[1,1,1,3,224,224]{5,4,3,2,1,0:T(8,128)(2,1)S(1)} collective-permute-done((bf16[1,1,1,3,224,224]{5,4,3,2,1,0:T(8,128)(2,1)S(1)}, bf16[1,1,1,3,224,224]{5,4,3,2,1,0:T(8,128)(2,1)S(1)}, u32[]{:S(2)}, u32[]{:S(2)}) %collective-permute-start) | collective-permute-done | bytes 301088 | tf_op jit(solution)/shard_map/ppermute | solution.py:369
  38.9 5.3 %patch_rows.2 = bf16[16,296,128]{2,1,0:T(8,128)(2,1)} custom-call(s32[1]{0:T(128)} %bitcast.3.valid_ref, s32[1,512]{1,0:T(1,128)} %bitcast.13, bf16[1,1,1,3,224,224]{5,4,3,2,1,0:T(8,128)(2,1)} %copy-done.6, bf16[1,1,4,3,224,224]{5,4,3,2,1,0:T(8,128)(2,1)} %fb_ref.3), custom_call_target="tpu_custom_call" | custom-call | tf_op jit(solution)/shard_map/patch_rows/pallas_call | solution.py:117
  44.2 13.1 %all-to-all-done.1.arr_ref = bf16[16,296,128]{2,1,0:T(8,128)(2,1)S(1)} async-done(((bf16[16,296,128]{2,1,0:T(8,128)(2,1)}), bf16[16,296,128]{2,1,0:T(8,128)(2,1)S(1)}, u32[]{:S(2)}, u32[]{:S(2)}) %all-to-all-start.1) | async-done | bytes 1212448 | tf_op jit(solution)/shard_map/all_to_all | solution.py:374
  57.3 3.8 %all-to-all-start = ((bf16[16,296,128]{2,1,0:T(8,128)(2,1)}), bf16[16,296,128]{2,1,0:T(8,128)(2,1)S(1)}, u32[]{:S(2)}, u32[]{:S(2)}) async-start(bf16[16,296,128]{2,1,0:T(8,128)(2,1)} %patch_rows.2), calls=%async_computation | async-start | bytes 2424832 | tf_op jit(solution)/shard_map/all_to_all | solution.py:377
  63.3 7.5 %first_half.1 = (bf16[512,640]{1,0:T(8,128)(2,1)}, f32[512,1280]{1,0:T(8,128)}) custom-call(s32[512,1]{1,0:T(8,128)} %copy.13.slot_ref, bf16[16,296,128]{2,1,0:T(8,128)(2,1)} %copy-done, bf16[1280,1280]{1,0:T(8,128)(2,1)} %all-gather.2.cloned.1.call-done.w_ref), custom_call_target="tpu_custom_call" | custom-call | tf_op jit(solution)/shard_map/first_half/pallas_call | solution.py:174
  70.8 21.5 %all-to-all-done.arr_ref = bf16[16,296,128]{2,1,0:T(8,128)(2,1)S(1)} async-done(((bf16[16,296,128]{2,1,0:T(8,128)(2,1)}), bf16[16,296,128]{2,1,0:T(8,128)(2,1)S(1)}, u32[]{:S(2)}, u32[]{:S(2)}) %all-to-all-start) | async-done | bytes 1212448 | tf_op jit(solution)/shard_map/all_to_all | solution.py:377
  93.4 10.7 %norm_backward.1 = (bf16[512,1280]{1,0:T(8,128)(2,1)}, bf16[512,640]{1,0:T(8,128)(2,1)}, bf16[512,640]{1,0:T(8,128)(2,1)}, f32[16,1280]{1,0:T(8,128)}) custom-call(s32[2]{0:T(128)} %pad_add_fusion.core_ref, s32[512,1]{1,0:T(8,128)} %copy.13.slot_ref, bf16[16,296,128]{2,1,0:T(8,128)(2,1)} %copy-done.1, bf16[512,640]{1,0:T(8,128)(2,1)} %get-tuple-element.16.rows0_ref, ...), custom_call_target="tpu_custom_call" | custom-call | tf_op jit(solution)/shard_map/norm_backward/pallas_call | solution.py:227
  104.5 3.7 %collective-permute-done.2.rows1_ref = bf16[512,640]{1,0:T(8,128)(2,1)S(1)} collective-permute-done((bf16[512,640]{1,0:T(8,128)(2,1)}, bf16[512,640]{1,0:T(8,128)(2,1)S(1)}, u32[]{:S(2)}, u32[]{:S(2)}) %collective-permute-start.2) | collective-permute-done | bytes 655392 | tf_op jit(solution)/shard_map/ppermute | solution.py:383
  109.5 7.2 %products.1 = (f32[1600,128]{1,0:T(8,128)}, bf16[1600,128]{1,0:T(8,128)(2,1)}, bf16[1600,128]{1,0:T(8,128)(2,1)}, bf16[1600,128]{1,0:T(8,128)(2,1)}) custom-call(s32[2]{0:T(128)} %pad_add_fusion.core_ref, bf16[512,1280]{1,0:T(8,128)(2,1)} %get-tuple-element.18.grad0_ref, bf16[512,1280]{1,0:T(8,128)(2,1)} %copy-done.3, ...), custom_call_target="tpu_custom_call" | custom-call | tf_op jit(solution)/shard_map/products/pallas_call | solution.py:276
  117.9 1.5 collective-permute-start.4
  119.4 1.5 collective-permute-start.5
  120.9 4.3 %collective-permute-done.3 = bf16[1600,128]{1,0:T(8,128)(2,1)S(1)} collective-permute-done((bf16[1600,128]{1,0:T(8,128)(2,1)}, bf16[1600,128]{1,0:T(8,128)(2,1)S(1)}, u32[]{:S(2)}, u32[]{:S(2)}) %collective-permute-start.3) | collective-permute-done | bytes 409632 | tf_op jit(solution)/shard_map/ppermute | solution.py:386
  125.2 3.8 %collective-permute-done.4 = bf16[1600,128]{1,0:T(8,128)(2,1)S(1)} collective-permute-done((bf16[1600,128]{1,0:T(8,128)(2,1)}, bf16[1600,128]{1,0:T(8,128)(2,1)S(1)}, u32[]{:S(2)}, u32[]{:S(2)}) %collective-permute-start.4) | collective-permute-done | bytes 409632 | tf_op jit(solution)/shard_map/ppermute | solution.py:386
  129.0 1.6 collective-permute-done.5
  131.9 12.3 %all_to_all.25 = f32[4,400,128]{2,1,0:T(8,128)S(1)} all-to-all(f32[4,400,128]{2,1,0:T(8,128)S(1)} %bitcast.10), channel_id=1, replica_groups={{0,4,8,12},{1,5,9,13},{2,6,10,14},{3,7,11,15},{16,17,18,19},{20,21,22,2..., dimensions={0} | all-to-all | bytes 1638400 | tf_op jit(solution)/shard_map/all_to_all | solution.py:390
  144.3 12.1 %all_to_all.26 = f32[8,56,128]{2,1,0:T(8,128)S(1)} all-to-all(f32[8,56,128]{2,1,0:T(8,128)S(1)} %bitcast.11), channel_id=1, replica_groups=mesh['z'=8,'core'=2,'slab'=4,'fsdp'=4] {'z'}, dimensions={0} | all-to-all | bytes 458752 | tf_op jit(solution)/shard_map/all_to_all | solution.py:394
  156.5 21.8 %all_to_all.27 = f32[32,56,128]{2,1,0:T(8,128)S(1)} all-to-all(f32[32,56,128]{2,1,0:T(8,128)S(1)} %broadcast_in_dim.13), channel_id=1, replica_groups=mesh['z'=8,'core'=2,'slab'=4,'fsdp'=4] {'slab','z'}, dimensions={0} | all-to-all | bytes 1835008 | tf_op jit(solution)/shard_map/all_to_all | solution.py:360
  178.3 8.2 %collective-permute-start.6 = (f32[1792,128]{1,0:T(8,128)S(1)}, f32[1792,128]{1,0:T(8,128)S(1)}, u32[]{:S(2)}, u32[]{:S(2)}) collective-permute-start(f32[1792,128]{1,0:T(8,128)S(1)} %bitcast.8), channel_id=1, source_target_pairs={{0,16},{16,0},{1,17},{17,1},{2,18},{18,2},{3,19},{19,3},{4,20},{20... | collective-permute-start | bytes 2752520 | tf_op jit(solution)/shard_map/ppermute | solution.py:396
  186.5 2.1 %collective-permute-done.6.other_ref = f32[1792,128]{1,0:T(8,128)S(1)} collective-permute-done((f32[1792,128]{1,0:T(8,128)S(1)}, f32[1792,128]{1,0:T(8,128)S(1)}, u32[]{:S(2)}, u32[]{:S(2)}) %collective-permute-start.6) | collective-permute-done | bytes 917536 | tf_op jit(solution)/shard_map/ppermute | solution.py:396
  189.5 3.6 %column_order.1 = (f32[320,1176]{1,0:T(8,128)}, f32[2,320]{1,0:T(2,128)}) custom-call(s32[2]{0:T(128)} %pad_add_fusion.core_ref, f32[1792,128]{1,0:T(8,128)} %bitcast.9, f32[1792,128]{1,0:T(8,128)} %copy-done.4), custom_call_target="tpu_custom_call" | custom-call | tf_op jit(solution)/shard_map/column_order/pallas_call | solution.py:328
  (34 shorter events, 10.4 us)
Async XLA Ops:
  7.2 56.1 %all-gather.2.cloned.1.call-start = ((), (), s32[]{:S(2)}) async-start(), calls=%async_computation.5 | async-start | bytes 4096000 | tf_op jit(solution)/shard_map/all_gather | solution.py:375
  16.1 41.2 %all-to-all-start.1 = ((bf16[16,296,128]{2,1,0:T(8,128)(2,1)}), bf16[16,296,128]{2,1,0:T(8,128)(2,1)S(1)}, u32[]{:S(2)}, u32[]{:S(2)}) async-start(bf16[16,296,128]{2,1,0:T(8,128)(2,1)} %patch_rows.3), calls=%async_computation.1 | async-start | bytes 2424832 | tf_op jit(solution)/shard_map/all_to_all | solution.py:374
  27.1 11.0 %collective-permute-start = (bf16[1,1,1,3,224,224]{5,4,3,2,1,0:T(8,128)(2,1)S(1)}, bf16[1,1,1,3,224,224]{5,4,3,2,1,0:T(8,128)(2,1)S(1)}, u32[]{:S(2)}, u32[]{:S(2)}) collective-permute-start(bf16[1,1,1,3,224,224]{5,4,3,2,1,0:T(8,128)(2,1)S(1)} %slice.3), channel_id=1, source_target_pairs={{0,4},{4,8},{8,12},{12,0},{1,5},{5,9},{9,13},{13,1},{2,6},{6,10},{... | collective-permute-start | bytes 903176 | tf_op jit(solution)/shard_map/ppermute | solution.py:369
  38.1 0.7 copy-start.6
  44.2 16.9 %copy-start.7 = (f32[1280]{0:T(1024)S(1)}, f32[1280]{0:T(1024)}, u32[]{:S(2)}) copy-start(f32[1280]{0:T(1024)} %param.12) | copy-start | bytes 15364
  44.2 17.5 %copy-start.8 = (s32[1,1,512]{2,1,0:T(1,128)S(1)}, s32[1,1,512]{2,1,0:T(1,128)}, u32[]{:S(2)}) copy-start(s32[1,1,512]{2,1,0:T(1,128)} %param.13) | copy-start | bytes 6148
  57.3 5.3 %copy-start = (bf16[16,296,128]{2,1,0:T(8,128)(2,1)}, bf16[16,296,128]{2,1,0:T(8,128)(2,1)S(1)}, u32[]{:S(2)}) copy-start(bf16[16,296,128]{2,1,0:T(8,128)(2,1)S(1)} %all-to-all-done.1.arr_ref) | copy-start | bytes 3637252
  57.3 35.0 %all-to-all-start = ((bf16[16,296,128]{2,1,0:T(8,128)(2,1)}), bf16[16,296,128]{2,1,0:T(8,128)(2,1)S(1)}, u32[]{:S(2)}, u32[]{:S(2)}) async-start(bf16[16,296,128]{2,1,0:T(8,128)(2,1)} %patch_rows.2), calls=%async_computation | async-start | bytes 2424832 | tf_op jit(solution)/shard_map/all_to_all | solution.py:377
  92.3 1.0 copy-start.1
  104.0 4.2 %collective-permute-start.1 = (bf16[512,1280]{1,0:T(8,128)(2,1)}, bf16[512,1280]{1,0:T(8,128)(2,1)S(1)}, u32[]{:S(2)}, u32[]{:S(2)}) collective-permute-start(bf16[512,1280]{1,0:T(8,128)(2,1)} %get-tuple-element.18.grad0_ref), channel_id=1, source_target_pairs={{0,16},{16,0},{1,17},{17,1},{2,18},{18,2},{3,19},{19,3},{4,20},{20... | collective-permute-start | bytes 3932168 | tf_op jit(solution)/shard_map/ppermute | solution.py:384
  104.0 4.2 %collective-permute-start.2 = (bf16[512,640]{1,0:T(8,128)(2,1)}, bf16[512,640]{1,0:T(8,128)(2,1)S(1)}, u32[]{:S(2)}, u32[]{:S(2)}) collective-permute-start(bf16[512,640]{1,0:T(8,128)(2,1)} %get-tuple-element.20), channel_id=1, source_target_pairs={{0,16},{16,0},{1,17},{17,1},{2,18},{18,2},{3,19},{19,3},{4,20},{20... | collective-permute-start | bytes 1966088 | tf_op jit(solution)/shard_map/ppermute | solution.py:383
  108.2 0.9 copy-start.5
  108.2 1.3 copy-start.3
  116.7 8.5 %collective-permute-start.3 = (bf16[1600,128]{1,0:T(8,128)(2,1)}, bf16[1600,128]{1,0:T(8,128)(2,1)S(1)}, u32[]{:S(2)}, u32[]{:S(2)}) collective-permute-start(bf16[1600,128]{1,0:T(8,128)(2,1)} %get-tuple-element.23), channel_id=1, source_target_pairs={{0,1},{16,20},{1,2},{17,21},{2,3},{18,22},{3,0},{19,23},{4,5},{20,... | collective-permute-start | bytes 1228808 | tf_op jit(solution)/shard_map/ppermute | solution.py:386
  117.9 11.1 %collective-permute-start.4 = (bf16[1600,128]{1,0:T(8,128)(2,1)}, bf16[1600,128]{1,0:T(8,128)(2,1)S(1)}, u32[]{:S(2)}, u32[]{:S(2)}) collective-permute-start(bf16[1600,128]{1,0:T(8,128)(2,1)} %get-tuple-element.24), channel_id=1, source_target_pairs={{0,3},{16,28},{1,0},{17,29},{2,1},{18,30},{3,2},{19,31},{4,7},{20,... | collective-permute-start | bytes 1228808 | tf_op jit(solution)/shard_map/ppermute | solution.py:386
  119.4 11.2 %collective-permute-start.5 = (bf16[1600,128]{1,0:T(8,128)(2,1)}, bf16[1600,128]{1,0:T(8,128)(2,1)S(1)}, u32[]{:S(2)}, u32[]{:S(2)}) collective-permute-start(bf16[1600,128]{1,0:T(8,128)(2,1)} %get-tuple-element.25), channel_id=1, source_target_pairs={{0,2},{16,24},{1,3},{17,25},{2,0},{18,26},{3,1},{19,27},{4,6},{20,... | collective-permute-start | bytes 1228808 | tf_op jit(solution)/shard_map/ppermute | solution.py:386
  178.3 10.3 %copy-start.2 = (f32[32,56,128]{2,1,0:T(8,128)}, f32[32,56,128]{2,1,0:T(8,128)S(1)}, u32[]{:S(2)}) copy-start(f32[32,56,128]{2,1,0:T(8,128)S(1)} %all_to_all.27) | copy-start | bytes 2752516
  178.3 10.3 %collective-permute-start.6 = (f32[1792,128]{1,0:T(8,128)S(1)}, f32[1792,128]{1,0:T(8,128)S(1)}, u32[]{:S(2)}, u32[]{:S(2)}) collective-permute-start(f32[1792,128]{1,0:T(8,128)S(1)} %bitcast.8), channel_id=1, source_target_pairs={{0,16},{16,0},{1,17},{17,1},{2,18},{18,2},{3,19},{19,3},{4,20},{20... | collective-permute-start | bytes 2752520 | tf_op jit(solution)/shard_map/ppermute | solution.py:396
  188.6 1.0 copy-start.4
Sparse Core Ops, SparseCore 0:
  16.2 47.0 all-gather.1

commit v4 on v3

--- a/solution.py
+++ b/solution.py
@@ -30,10 +30,10 @@
 PIECE = 56
 BLOCK = 128
 SUMS = 96
-VMEM = 60 * 1024 * 1024
 ALL = pl.BlockSpec(memory_space=pltpu.VMEM)
 SCALAR = pl.BlockSpec(memory_space=pltpu.SMEM)
-PARAMS = pltpu.CompilerParams(vmem_limit_bytes=VMEM)
+PARAMS = pltpu.CompilerParams(vmem_limit_bytes=24 * 1024 * 1024)
+WIDE = pltpu.CompilerParams(vmem_limit_bytes=60 * 1024 * 1024)
 LANES = (((1,), (1,)), ((), ()))
 SUBLANES = (((0,), (0,)), ((), ()))
 
@@ -129,24 +129,35 @@
             pltpu.VMEM((2, COLOURS, 2, SIDE, 128), jnp.float32),
             pltpu.VMEM((ROWS, HALF), jnp.bfloat16),
         ],
-        compiler_params=PARAMS,
+        compiler_params=WIDE,
         name="patch_rows",
     )(valid, slots, first, second)
 
 
-def weight_kernel(place_ref, w_ref, out_ref):
+def weight_kernel(place_ref, column_ref, own_ref, *refs):
+    *parts, out_ref, held_ref = refs
+    core, y = place_ref[0], place_ref[2]
+    part = OWNED // 2
+    held_ref[pl.ds(pl.multiple_of(y * OWNED, 16), OWNED), :] = own_ref[...]
+    for n, ref in enumerate(parts):
+        side, by = divmod(n, 3)
+        row = ((y - by - 1) & 3) * OWNED + (core if side == 0 else 1 - core) * part
+        held_ref[pl.ds(pl.multiple_of(row, 16), part), :] = ref[...]
     for i in range(2):
-        pick = one_hot(iota((HALF, KIN), 0) + i * HALF == place_ref[...])
-        out_ref[:, i * HALF : (i + 1) * HALF] = dot(w_ref[...], pick, LANES).astype(jnp.bfloat16)
-
-
-def padded_weight(weight):
+        pick = one_hot(iota((HALF, KIN), 0) + i * HALF == column_ref[...])
+        out_ref[:, i * HALF : (i + 1) * HALF] = dot(held_ref[...], pick, LANES).astype(jnp.bfloat16)
+
+
+def padded_weight(place, own, parts):
     return pl.pallas_call(
         weight_kernel,
-        out_shape=jax.ShapeDtypeStruct((weight.shape[0], 2 * HALF), jnp.bfloat16),
-        compiler_params=PARAMS,
+        out_shape=jax.ShapeDtypeStruct((D, 2 * HALF), jnp.bfloat16),
+        in_specs=[SCALAR] + [ALL] * 8,
+        out_specs=ALL,
+        scratch_shapes=[pltpu.VMEM((D, KIN), jnp.bfloat16)],
+        compiler_params=WIDE,
         name="weight_columns",
-    )(jnp.asarray(column_places()), weight)
+    )(place, jnp.asarray(column_places()), own, *parts)
 
 
 def taken_rows(slot_ref, arr_ref, cols_ref):
@@ -180,50 +191,51 @@
         in_specs=[ALL] * 3,
         out_specs=(ALL, ALL),
         scratch_shapes=[pltpu.VMEM((HALF, PEERS * CAP), jnp.bfloat16)],
-        compiler_params=PARAMS,
+        compiler_params=WIDE,
         name="first_half",
     )(slots, arrived, weight)
 
 
 def backward_kernel(core_ref, slot_ref, arr_ref, rows0_ref, part_ref, w_ref, g_ref, r_ref, gain_ref, grad_ref, mine_ref, send_ref, sums_ref, cols_ref, rows1_ref):
-    rows1_ref[...] = taken_rows(slot_ref, arr_ref, cols_ref)
+    step = pl.program_id(0)
+
+    @pl.when(step == 0)
+    def _():
+        rows1_ref[...] = taken_rows(slot_ref, arr_ref, cols_ref)
+        sums_ref[...] = jnp.zeros_like(sums_ref)
+
+    here = pl.ds(pl.multiple_of(step * BLOCK, BLOCK), BLOCK)
 
     @pl.when(core_ref[0] == 0)
     def _():
         mine_ref[...] = rows0_ref[...]
-        send_ref[...] = rows1_ref[...]
+        send_ref[...] = rows1_ref[here, :]
 
     @pl.when(core_ref[0] != 0)
     def _():
-        mine_ref[...] = rows1_ref[...]
+        mine_ref[...] = rows1_ref[here, :]
         send_ref[...] = rows0_ref[...]
 
-    gain = gain_ref[...]
-    gain_sums = jnp.zeros((8, D), jnp.float32)
-    bias_sums = jnp.zeros((8, D), jnp.float32)
-    for i in range(ROWS // BLOCK):
-        here = slice(i * BLOCK, (i + 1) * BLOCK)
-        embedded = part_ref[here, :] + dot(rows1_ref[here, :], w_ref[:, HALF:], LANES)
-        deviation = embedded - jnp.mean(embedded, axis=-1, keepdims=True)
-        variance = jnp.mean(deviation * deviation, axis=-1, keepdims=True)
-        inverse_std = lax.rsqrt(variance + 1e-06)
-        normalized = deviation * inverse_std
-        upstream_norm = g_ref[0, 0, here, :].astype(jnp.float32)
-        upstream = upstream_norm * gain
-        inner = jnp.mean(upstream * normalized, axis=-1, keepdims=True)
-        level = jnp.mean(upstream, axis=-1, keepdims=True)
-        input_grad = r_ref[0, 0, here, :].astype(jnp.float32) + inverse_std * (
-            upstream - level - normalized * inner
-        )
-        grad_ref[here, :] = input_grad.astype(jnp.bfloat16)
-        gain_sums += jnp.sum((upstream_norm * normalized).reshape(BLOCK // 8, 8, D), axis=0)
-        bias_sums += jnp.sum(upstream_norm.reshape(BLOCK // 8, 8, D), axis=0)
-    sums_ref[0:8, :] = gain_sums
-    sums_ref[8:16, :] = bias_sums
+    embedded = part_ref[...] + dot(rows1_ref[here, :], w_ref[...], LANES)
+    deviation = embedded - jnp.mean(embedded, axis=-1, keepdims=True)
+    variance = jnp.mean(deviation * deviation, axis=-1, keepdims=True)
+    inverse_std = lax.rsqrt(variance + 1e-06)
+    normalized = deviation * inverse_std
+    upstream_norm = g_ref[0, 0].astype(jnp.float32)
+    upstream = upstream_norm * gain_ref[...]
+    inner = jnp.mean(upstream * normalized, axis=-1, keepdims=True)
+    level = jnp.mean(upstream, axis=-1, keepdims=True)
+    input_grad = r_ref[0, 0].astype(jnp.float32) + inverse_std * (upstream - level - normalized * inner)
+    grad_ref[...] = input_grad.astype(jnp.bfloat16)
+    sums_ref[0:8, :] += jnp.sum((upstream_norm * normalized).reshape(BLOCK // 8, 8, D), axis=0)
+    sums_ref[8:16, :] += jnp.sum(upstream_norm.reshape(BLOCK // 8, 8, D), axis=0)
 
 
 def norm_backward(core, slots, arrived, rows0, part, weight, grad_norm, grad_resid, gain):
     half = jax.ShapeDtypeStruct((ROWS, HALF), jnp.bfloat16)
+    packed = pl.BlockSpec((1, 1, BLOCK, D), lambda i: (0, 0, i, 0))
+    rows = pl.BlockSpec((BLOCK, D), lambda i: (i, 0))
+    halves = pl.BlockSpec((BLOCK, HALF), lambda i: (i, 0))
     return pl.pallas_call(
         backward_kernel,
         out_shape=(
@@ -232,18 +244,29 @@
             half,
             jax.ShapeDtypeStruct((16, D), jnp.float32),
         ),
-        in_specs=[SCALAR] + [ALL] * 8,
-        out_specs=(ALL,) * 4,
+        grid=(ROWS // BLOCK,),
+        in_specs=[
+            SCALAR,
+            pl.BlockSpec((ROWS, 1), lambda i: (0, 0)),
+            pl.BlockSpec((PEERS, HELD, 128), lambda i: (0, 0, 0)),
+            halves,
+            rows,
+            pl.BlockSpec((D, HALF), lambda i: (0, 1)),
+            packed,
+            packed,
+            pl.BlockSpec((1, D), lambda i: (0, 0)),
+        ],
+        out_specs=(rows, halves, halves, pl.BlockSpec((16, D), lambda i: (0, 0))),
         scratch_shapes=[
             pltpu.VMEM((HALF, PEERS * CAP), jnp.bfloat16),
             pltpu.VMEM((ROWS, HALF), jnp.bfloat16),
         ],
-        compiler_params=PARAMS,
+        compiler_params=WIDE,
         name="norm_backward",
     )(core, slots, arrived, rows0, part, weight, grad_norm, grad_resid, gain)
 
 
-def product_kernel(core_ref, grad0_ref, grad1_ref, rows0_ref, rows1_ref, sums_ref, own_ref, out1_ref, out2_ref, out3_ref, terms_ref):
+def product_kernel(core_ref, grad0_ref, grad1_ref, rows0_ref, rows1_ref, sums_ref, own_ref, out1_ref, out2_ref, out3_ref, terms_ref, order_ref):
     core, place = core_ref[0], core_ref[1]
     kind = iota((128, HALF), 0)
     for i in range(D // HALF):
@@ -263,12 +286,10 @@
                 to = jnp.where(core == 0, y, o // 5)
                 at = jnp.where(core == 0, o * STEP, y * QUARTER + o % 5 * STEP)
                 at = pl.ds(pl.multiple_of(at, 16), STEP)
-                by = (to - place) & 3
-                for n_by, ref in enumerate((own_ref, out1_ref, out2_ref, out3_ref)):
-
-                    @pl.when(by == n_by)
-                    def _(ref=ref, at=at, block=block):
-                        ref[at, :] = block.astype(ref.dtype)
+                order_ref[(to - place) & 3, at, :] = block
+    own_ref[...] = order_ref[0]
+    for by, ref in enumerate((out1_ref, out2_ref, out3_ref)):
+        ref[...] = order_ref[by + 1].astype(jnp.bfloat16)
 
 
 def products(core, grad0, grad1, rows0, rows1, sums):
@@ -278,7 +299,10 @@
         out_shape=(jax.ShapeDtypeStruct((LINE, 128), jnp.float32), sent, sent, sent),
         in_specs=[SCALAR] + [ALL] * 5,
         out_specs=(ALL,) * 4,
-        scratch_shapes=[pltpu.VMEM((HALF, HALF), jnp.float32)],
+        scratch_shapes=[
+            pltpu.VMEM((HALF, HALF), jnp.float32),
+            pltpu.VMEM((4, LINE, 128), jnp.float32),
+        ],
         compiler_params=PARAMS,
         name="products",
     )(core, grad0, grad1, rows0, rows1, sums)
@@ -300,12 +324,8 @@
 def finish_kernel(core_ref, mine_ref, other_ref, out_ref, norm_ref, held_ref, last_ref):
     core = core_ref[0]
     for t in range(TILES):
-        for r in range(OWNED // STEP):
-            x, w = divmod(t * (OWNED // STEP) + r, 5)
-            source = slice(x * 8 * PIECE + w * STEP, x * 8 * PIECE + (w + 1) * STEP)
-            at = slice(r * STEP, (r + 1) * STEP)
-            held_ref[core * TILES + t, at, :] = mine_ref[source, :]
-            held_ref[(1 - core) * TILES + t, at, :] = other_ref[source, :]
+        held_ref[core * TILES + t] = mine_ref[t * OWNED : (t + 1) * OWNED, :]
+        held_ref[(1 - core) * TILES + t] = other_ref[t * OWNED : (t + 1) * OWNED, :]
     lane = iota((OWNED, 128), 1)
     for tile in range(pl.cdiv(KIN, 128)):
         acc = None
@@ -365,21 +385,25 @@
     core = lax.axis_index("core").astype(jnp.int32)
     x = lax.axis_index("slab").astype(jnp.int32)
     y = lax.axis_index("fsdp").astype(jnp.int32)
-    place = jnp.stack([core, jnp.where(core == 0, y, x)])
+    place = jnp.stack([core, jnp.where(core == 0, y, x), y])
     earlier = lax.ppermute(pixels[:, :, 3:4], "slab", [(i, (i + 1) % 4) for i in range(4)])
     takes = recv_slot.reshape(1, ROWS)
     sends = send_slot.reshape(ROWS, 1)
     packed0 = packed_rows(jnp.ones((1,), jnp.int32), takes, pixels, pixels, 0, 2)
-    packed0, embed_weight = lax.optimization_barrier((packed0, embed_weight))
+    packed0, shard = lax.optimization_barrier((packed0, embed_weight))
     arrived0 = lax.all_to_all(packed0, ("z", "core"), 0, 0, tiled=True)
-    weight = lax.all_gather(padded_weight(embed_weight), "fsdp", axis=0, tiled=True)
+    swap = [(0, 1), (1, 0)]
+    part = lax.dynamic_slice_in_dim(shard, core * (OWNED // 2), OWNED // 2, 0)
+    parts = [lax.ppermute(part, "fsdp", [(i, (i + by) % 4) for i in range(4)]) for by in (1, 2, 3)]
+    earlier, *parts = lax.optimization_barrier((earlier, *parts))
     packed1 = packed_rows((x > 0).astype(jnp.int32)[None], takes, earlier, pixels, 0, 1)
     arrived1 = lax.all_to_all(packed1, ("z", "core"), 0, 0, tiled=True)
+    parts += [lax.ppermute(part, "core", swap) for part in parts]
+    weight = padded_weight(place, embed_weight, parts)
     rows0, part = first_half(sends, arrived0, weight)
     grads, mine, send, sums = norm_backward(
         place, sends, arrived1, rows0, part, weight, grad_norm, grad_resid, norm_gain.reshape(1, D)
     )
-    swap = [(0, 1), (1, 0)]
     theirs = lax.ppermute(send, "core", swap)
     their_grads = lax.ppermute(grads, "core", swap)
     own, *sent = products(place, grads, their_grads, mine, theirs, sums)
@@ -392,7 +416,8 @@
     )
     quarter = jnp.pad(jnp.sum(quarters, axis=0), ((0, 8 * PIECE - QUARTER), (0, 0)))
     pieces = lax.all_to_all(quarter.reshape(8, PIECE, 128), "z", 0, 0, tiled=True)
-    line = copies(jnp.sum(pieces, axis=0), ("slab", "z"), 32).reshape(32 * PIECE, 128)
+    quarter = copies(jnp.sum(pieces, axis=0), "z", 8).reshape(8 * PIECE, 128)[:QUARTER]
+    line = copies(quarter, "slab", 4).reshape(LINE, 128)
     return finish(place, line, lax.ppermute(line, "core", swap))
 
 

time: 201 us -> 178 us (0.89)
  waiting for transfers between devices: 59.8 us -> 46.2 us
  between operations: 14.1 us -> 0.74 us
  starting transfers between devices: 28 us -> 33 us
    all_to_all x1, waiting for transfers between devices: 13.1 us -> 1.16 us  [shards(): arrived0 = lax.all_to_all(packed0, ('z', 'core'), 0, 0, tiled=True)]
    ppermute x0 -> x6, waiting for transfers between devices: none -> 9.89 us  [the longest x3 9.68 us: shards(): lax.ppermute(part, 'fsdp', [(i, (i + by) % 4) for i in range(4)])]
    all_to_all x1, waiting for transfers between devices: 21.5 us -> 11.6 us  [shards(): arrived1 = lax.all_to_all(packed1, ('z', 'core'), 0, 0, tiled=True)]
    pallas_call x1, Pallas kernels: 3.57 us -> 9.02 us  [padded_weight(): pl.pallas_call(weight_kernel, out_shape=jax.ShapeDtypeStruct((D, 2 * HALF...]
    ppermute x0 -> x6, starting transfers between devices: none -> 4.67 us  [the longest x3 3.89 us: shards(): lax.ppermute(part, 'fsdp', [(i, (i + by) % 4) for i in range(4)])]
    pallas_call x1, Pallas kernels: 7.21 us -> 3.16 us  [products(): pl.pallas_call(product_kernel, out_shape=(jax.ShapeDtypeStruct((LINE, 128...]
    all_to_all x1, starting transfers between devices: 3.78 us -> 6.2 us  [shards(): arrived1 = lax.all_to_all(packed1, ('z', 'core'), 0, 0, tiled=True)]
    ppermute x1, starting transfers between devices: 8.16 us -> 5.87 us  [shards(): return finish(place, line, lax.ppermute(line, 'core', swap))]
  transfers between devices with their start and end apart: 10 -> 15, of which waited for: 9 -> 11; matrix products, arithmetic and copies ran while one was open for 2% -> 2% of each run, Pallas kernels for 6% -> 12%
where the time goes in v4:
time: 178 us; the launch traced here: 177 us
  blocking collectives  46.3 us (26%)
  waiting for transfers between devices  46.2 us (26%)
  Pallas kernels  42.9 us (24%)
  starting transfers between devices  33 us (19%)
  local copies, waits for them, and re-layouts  6.96 us (4%)
    all_to_all x2, blocking collectives, copies(): return lax.all_to_all(array, axis, 0, 0, tiled=True)  23.5 us
    all_to_all x1, waiting for transfers between devices, shards(): arrived1 = lax.all_to_all(packed1, ('z', 'core'), 0, 0, tiled=True)  11.6 us
    all_to_all x1, blocking collectives, shards(): lax.all_to_all(quarter.reshape(8, PIECE, 128), 'z', 0, 0, tiled=True)  11.6 us
    all_to_all x1, blocking collectives, shards(): lax.all_to_all(line.reshape(4, QUARTER, 128), plane, 0, 0, tiled=True, ax...  11.2 us
    pallas_call x2, Pallas kernels, packed_rows(): pl.pallas_call(patch_kernel, out_shape=jax.ShapeDtypeStruct(shape, jnp.bf...  10.8 us
    all_to_all x1, starting transfers between devices, shards(): arrived0 = lax.all_to_all(packed0, ('z', 'core'), 0, 0, tiled=True)  10.1 us
    pallas_call x1, Pallas kernels, norm_backward(): pl.pallas_call(backward_kernel, out_shape=(jax.ShapeDtypeStruct((ROWS, D)...  9.7 us
    ppermute x3, waiting for transfers between devices, shards(): lax.ppermute(part, 'fsdp', [(i, (i + by) % 4) for i in range(4)])  9.68 us
  transfers between devices with their start and end apart: 15, of which 11 were waited for; matrix products, arithmetic and copies ran while one was open for 2% of the time, Pallas kernels for 12%

profile of v4, /device:TPU:1, one launch (start us, length us, event | category | flops | bytes accessed | tf_op | source)
XLA Modules:
  0.0 176.9 jit_solution(4251395344607883523)
XLA Ops:
  0.6 5.3 %patch_rows.2 = bf16[16,296,128]{2,1,0:T(8,128)(2,1)} custom-call(s32[1]{0:T(128)} %constant.22.clone.1.valid_ref, s32[1,512]{1,0:T(1,128)} %bitcast.15, bf16[1,1,4,3,224,224]{5,4,3,2,1,0:T(8,128)(2,1)} %fb_ref.3, bf16[1,1,4,3,224,224]{5,4,3,2,1,0:T(8,128)(2,1)} %fb_ref.3), custom_call_target="tpu_custom_call" | custom-call | tf_op jit(solution)/shard_map/patch_rows/pallas_call | solution.py:117
  6.0 10.1 %all-to-all-start.1 = ((bf16[16,296,128]{2,1,0:T(8,128)(2,1)}), bf16[16,296,128]{2,1,0:T(8,128)(2,1)S(1)}, u32[]{:S(2)}, u32[]{:S(2)}) async-start(bf16[16,296,128]{2,1,0:T(8,128)(2,1)} %patch_rows.2), calls=%async_computation.1 | async-start | bytes 2424832 | tf_op jit(solution)/shard_map/all_to_all | solution.py:394
  16.1 2.8 %collective-permute-start.3 = (bf16[160,1176]{1,0:T(8,128)(2,1)S(1)}, bf16[160,1176]{1,0:T(8,128)(2,1)S(1)}, u32[]{:S(2)}, u32[]{:S(2)}) collective-permute-start(bf16[160,1176]{1,0:T(8,128)(2,1)S(1)} %constant_dynamic-slice_fusion), channel_id=1, source_target_pairs={{0,3},{1,0},{2,1},{3,2},{4,7},{5,4},{6,5},{7,6},{8,11},{9,8},{10,9... | collective-permute-start | bytes 1128968 | tf_op jit(solution)/shard_map/ppermute | solution.py:397
  22.3 8.7 %collective-permute-done.fa_ref = bf16[1,1,1,3,224,224]{5,4,3,2,1,0:T(8,128)(2,1)S(1)} collective-permute-done((bf16[1,1,1,3,224,224]{5,4,3,2,1,0:T(8,128)(2,1)S(1)}, bf16[1,1,1,3,224,224]{5,4,3,2,1,0:T(8,128)(2,1)S(1)}, u32[]{:S(2)}, u32[]{:S(2)}) %collective-permute-start) | collective-permute-done | bytes 301088 | tf_op jit(solution)/shard_map/ppermute | solution.py:389
  31.0 5.5 %collective-permute-done.3.refs_2_ = bf16[160,1176]{1,0:T(8,128)(2,1)S(1)} collective-permute-done((bf16[160,1176]{1,0:T(8,128)(2,1)S(1)}, bf16[160,1176]{1,0:T(8,128)(2,1)S(1)}, u32[]{:S(2)}, u32[]{:S(2)}) %collective-permute-start.3) | collective-permute-done | bytes 376352 | tf_op jit(solution)/shard_map/ppermute | solution.py:397
  36.4 4.2 %collective-permute-done.1.refs_0_ = bf16[160,1176]{1,0:T(8,128)(2,1)S(1)} collective-permute-done((bf16[160,1176]{1,0:T(8,128)(2,1)S(1)}, bf16[160,1176]{1,0:T(8,128)(2,1)S(1)}, u32[]{:S(2)}, u32[]{:S(2)}) %collective-permute-start.1) | collective-permute-done | bytes 376352 | tf_op jit(solution)/shard_map/ppermute | solution.py:397
  40.6 5.5 %patch_rows.3 = bf16[16,296,128]{2,1,0:T(8,128)(2,1)} custom-call(s32[1]{0:T(128)} %bitcast.4.valid_ref, s32[1,512]{1,0:T(1,128)} %bitcast.16, bf16[1,1,1,3,224,224]{5,4,3,2,1,0:T(8,128)(2,1)} %copy-done.10, bf16[1,1,4,3,224,224]{5,4,3,2,1,0:T(8,128)(2,1)} %fb_ref.3), custom_call_target="tpu_custom_call" | custom-call | tf_op jit(solution)/shard_map/patch_rows/pallas_call | solution.py:117
  47.3 6.2 %all-to-all-start = ((bf16[16,296,128]{2,1,0:T(8,128)(2,1)}), bf16[16,296,128]{2,1,0:T(8,128)(2,1)S(1)}, u32[]{:S(2)}, u32[]{:S(2)}) async-start(bf16[16,296,128]{2,1,0:T(8,128)(2,1)} %patch_rows.3), calls=%async_computation | async-start | bytes 2424832 | tf_op jit(solution)/shard_map/all_to_all | solution.py:400
  56.6 9.0 %weight_columns.1.w_ref = bf16[1280,1280]{1,0:T(8,128)(2,1)} custom-call(s32[3]{0:T(128)} %pad_add_fusion.place_ref.core_ref, s32[1,1176]{1,0:T(1,128)} %constant.26.clone.column_ref, bf16[320,1176]{1,0:T(8,128)(2,1)} %own_ref.1, bf16[160,1176]{1,0:T(8,128)(2,1)} %copy-done.9, bf16[160,1176]{1,0:T(8,128)(2,1)} %copy-done.8, bf16[160,1176]{1,0:T(8,128)(2,1)} %copy-done.7, ...), custom_call_target="tpu_custom_call" | custom-call | tf_op jit(solution)/shard_map/weight_columns/pallas_call | solution.py:152
  65.6 7.5 %first_half.1 = (bf16[512,640]{1,0:T(8,128)(2,1)}, f32[512,1280]{1,0:T(8,128)}) custom-call(s32[512,1]{1,0:T(8,128)} %copy.13.slot_ref, bf16[16,296,128]{2,1,0:T(8,128)(2,1)} %copy-done.4, bf16[1280,1280]{1,0:T(8,128)(2,1)} %weight_columns.1.w_ref), custom_call_target="tpu_custom_call" | custom-call | tf_op jit(solution)/shard_map/first_half/pallas_call | solution.py:185
  73.1 11.6 %all-to-all-done.arr_ref = bf16[16,296,128]{2,1,0:T(8,128)(2,1)S(1)} async-done(((bf16[16,296,128]{2,1,0:T(8,128)(2,1)}), bf16[16,296,128]{2,1,0:T(8,128)(2,1)S(1)}, u32[]{:S(2)}, u32[]{:S(2)}) %all-to-all-start) | async-done | bytes 1212448 | tf_op jit(solution)/shard_map/all_to_all | solution.py:400
  85.8 9.7 %norm_backward.1 = (bf16[512,1280]{1,0:T(8,128)(2,1)}, bf16[512,640]{1,0:T(8,128)(2,1)}, bf16[512,640]{1,0:T(8,128)(2,1)}, f32[16,1280]{1,0:T(8,128)}) custom-call(s32[3]{0:T(128)} %pad_add_fusion.place_ref.core_ref, s32[512,1]{1,0:T(8,128)} %copy.13.slot_ref, bf16[16,296,128]{2,1,0:T(8,128)(2,1)} %copy-done.5, ...), custom_call_target="tpu_custom_call" | custom-call | tf_op jit(solution)/shard_map/norm_backward/pallas_call | solution.py:239
  96.1 3.7 %collective-permute-done.8.rows1_ref = bf16[512,640]{1,0:T(8,128)(2,1)S(1)} collective-permute-done((bf16[512,640]{1,0:T(8,128)(2,1)}, bf16[512,640]{1,0:T(8,128)(2,1)S(1)}, u32[]{:S(2)}, u32[]{:S(2)}) %collective-permute-start.8) | collective-permute-done | bytes 655392 | tf_op jit(solution)/shard_map/ppermute | solution.py:407
  103.1 3.2 %products.1 = (f32[1600,128]{1,0:T(8,128)S(1)}, bf16[1600,128]{1,0:T(8,128)(2,1)S(1)}, bf16[1600,128]{1,0:T(8,128)(2,1)S(1)}, bf16[1600,128]{1,0:T(8,128)(2,1)S(1)}) custom-call(s32[3]{0:T(128)S(1)} %copy-done.3, bf16[512,1280]{1,0:T(8,128)(2,1)S(1)} %copy-done, bf16[512,1280]{1,0:T(8,128)(2,1)S(1)} %collective-permute-done.7.grad1_ref, ...), custom_call_target="tpu_custom_call" | custom-call | tf_op jit(solution)/shard_map/products/pallas_call | solution.py:297
  107.5 1.5 collective-permute-start.10
  110.5 4.1 %collective-permute-done.9 = bf16[1600,128]{1,0:T(8,128)(2,1)S(1)} collective-permute-done((bf16[1600,128]{1,0:T(8,128)(2,1)S(1)}, bf16[1600,128]{1,0:T(8,128)(2,1)S(1)}, u32[]{:S(2)}, u32[]{:S(2)}) %collective-permute-start.9) | collective-permute-done | bytes 409632 | tf_op jit(solution)/shard_map/ppermute | solution.py:410
  114.6 3.7 %collective-permute-done.10 = bf16[1600,128]{1,0:T(8,128)(2,1)S(1)} collective-permute-done((bf16[1600,128]{1,0:T(8,128)(2,1)S(1)}, bf16[1600,128]{1,0:T(8,128)(2,1)S(1)}, u32[]{:S(2)}, u32[]{:S(2)}) %collective-permute-start.10) | collective-permute-done | bytes 409632 | tf_op jit(solution)/shard_map/ppermute | solution.py:410
  119.8 11.2 %all_to_all.30 = f32[4,400,128]{2,1,0:T(8,128)S(1)} all-to-all(f32[4,400,128]{2,1,0:T(8,128)S(1)} %bitcast.12), channel_id=1, replica_groups={{0,4,8,12},{1,5,9,13},{2,6,10,14},{3,7,11,15},{16,17,18,19},{20,21,22,2..., dimensions={0} | all-to-all | bytes 1638400 | tf_op jit(solution)/shard_map/all_to_all | solution.py:414
  131.1 11.6 %all_to_all.31 = f32[8,56,128]{2,1,0:T(8,128)S(1)} all-to-all(f32[8,56,128]{2,1,0:T(8,128)S(1)} %bitcast.13), channel_id=1, replica_groups=mesh['z'=8,'core'=2,'slab'=4,'fsdp'=4] {'z'}, dimensions={0} | all-to-all | bytes 458752 | tf_op jit(solution)/shard_map/all_to_all | solution.py:418
  142.8 11.4 %all_to_all.32 = f32[8,56,128]{2,1,0:T(8,128)S(1)} all-to-all(f32[8,56,128]{2,1,0:T(8,128)S(1)} %broadcast_in_dim.19), channel_id=1, replica_groups=mesh['z'=8,'core'=2,'slab'=4,'fsdp'=4] {'z'}, dimensions={0} | all-to-all | bytes 458752 | tf_op jit(solution)/shard_map/all_to_all | solution.py:380
  154.2 12.1 %all_to_all.33 = f32[4,400,128]{2,1,0:T(8,128)S(1)} all-to-all(f32[4,400,128]{2,1,0:T(8,128)S(1)} %broadcast_in_dim.20), channel_id=1, replica_groups=mesh['z'=8,'core'=2,'slab'=4,'fsdp'=4] {'slab'}, dimensions={0} | all-to-all | bytes 1638400 | tf_op jit(solution)/shard_map/all_to_all | solution.py:380
  166.3 5.9 %collective-permute-start.12 = (f32[1600,128]{1,0:T(8,128)S(1)}, f32[1600,128]{1,0:T(8,128)S(1)}, u32[]{:S(2)}, u32[]{:S(2)}) collective-permute-start(f32[1600,128]{1,0:T(8,128)S(1)} %bitcast.10), channel_id=1, source_target_pairs={{0,16},{16,0},{1,17},{17,1},{2,18},{18,2},{3,19},{19,3},{4,20},{20... | collective-permute-start | bytes 2457608 | tf_op jit(solution)/shard_map/ppermute | solution.py:421
  172.2 2.0 %collective-permute-done.12.other_ref = f32[1600,128]{1,0:T(8,128)S(1)} collective-permute-done((f32[1600,128]{1,0:T(8,128)S(1)}, f32[1600,128]{1,0:T(8,128)S(1)}, u32[]{:S(2)}, u32[]{:S(2)}) %collective-permute-start.12) | collective-permute-done | bytes 819232 | tf_op jit(solution)/shard_map/ppermute | solution.py:421
  174.1 2.7 %column_order.1 = (f32[320,1176]{1,0:T(8,128)}, f32[2,320]{1,0:T(2,128)}) custom-call(s32[3]{0:T(128)S(1)} %copy-done.3, f32[1600,128]{1,0:T(8,128)S(1)} %bitcast.11, f32[1600,128]{1,0:T(8,128)S(1)} %collective-permute-done.12.other_ref), custom_call_target="tpu_custom_call" | custom-call | tf_op jit(solution)/shard_map/column_order/pallas_call | solution.py:348
  (55 shorter events, 17.0 us)
Async XLA Ops:
  6.0 10.1 %copy-start.6 = (bf16[320,1176]{1,0:T(8,128)(2,1)S(1)}, bf16[320,1176]{1,0:T(8,128)(2,1)}, u32[]{:S(2)}) copy-start(bf16[320,1176]{1,0:T(8,128)(2,1)} %own_ref.1) | copy-start | bytes 2257924
  6.0 41.3 %all-to-all-start.1 = ((bf16[16,296,128]{2,1,0:T(8,128)(2,1)}), bf16[16,296,128]{2,1,0:T(8,128)(2,1)S(1)}, u32[]{:S(2)}, u32[]{:S(2)}) async-start(bf16[16,296,128]{2,1,0:T(8,128)(2,1)} %patch_rows.2), calls=%async_computation.1 | async-start | bytes 2424832 | tf_op jit(solution)/shard_map/all_to_all | solution.py:394
  16.1 20.3 %collective-permute-start.3 = (bf16[160,1176]{1,0:T(8,128)(2,1)S(1)}, bf16[160,1176]{1,0:T(8,128)(2,1)S(1)}, u32[]{:S(2)}, u32[]{:S(2)}) collective-permute-start(bf16[160,1176]{1,0:T(8,128)(2,1)S(1)} %constant_dynamic-slice_fusion), channel_id=1, source_target_pairs={{0,3},{1,0},{2,1},{3,2},{4,7},{5,4},{6,5},{7,6},{8,11},{9,8},{10,9... | collective-permute-start | bytes 1128968 | tf_op jit(solution)/shard_map/ppermute | solution.py:397
  19.0 17.4 %collective-permute-start.2 = (bf16[160,1176]{1,0:T(8,128)(2,1)S(1)}, bf16[160,1176]{1,0:T(8,128)(2,1)S(1)}, u32[]{:S(2)}, u32[]{:S(2)}) collective-permute-start(bf16[160,1176]{1,0:T(8,128)(2,1)S(1)} %constant_dynamic-slice_fusion), channel_id=1, source_target_pairs={{0,2},{1,3},{2,0},{3,1},{4,6},{5,7},{6,4},{7,5},{8,10},{9,11},{10,... | collective-permute-start | bytes 1128968 | tf_op jit(solution)/shard_map/ppermute | solution.py:397
  19.3 21.3 %collective-permute-start.1 = (bf16[160,1176]{1,0:T(8,128)(2,1)S(1)}, bf16[160,1176]{1,0:T(8,128)(2,1)S(1)}, u32[]{:S(2)}, u32[]{:S(2)}) collective-permute-start(bf16[160,1176]{1,0:T(8,128)(2,1)S(1)} %constant_dynamic-slice_fusion), channel_id=1, source_target_pairs={{0,1},{1,2},{2,3},{3,0},{4,5},{5,6},{6,7},{7,4},{8,9},{9,10},{10,1... | collective-permute-start | bytes 1128968 | tf_op jit(solution)/shard_map/ppermute | solution.py:397
  21.0 9.9 %collective-permute-start = (bf16[1,1,1,3,224,224]{5,4,3,2,1,0:T(8,128)(2,1)S(1)}, bf16[1,1,1,3,224,224]{5,4,3,2,1,0:T(8,128)(2,1)S(1)}, u32[]{:S(2)}, u32[]{:S(2)}) collective-permute-start(bf16[1,1,1,3,224,224]{5,4,3,2,1,0:T(8,128)(2,1)S(1)} %slice.6), channel_id=1, source_target_pairs={{0,4},{4,8},{8,12},{12,0},{1,5},{5,9},{9,13},{13,1},{2,6},{6,10},{... | collective-permute-start | bytes 903176 | tf_op jit(solution)/shard_map/ppermute | solution.py:389
  31.0 9.7 %copy-start.10 = (bf16[1,1,1,3,224,224]{5,4,3,2,1,0:T(8,128)(2,1)}, bf16[1,1,1,3,224,224]{5,4,3,2,1,0:T(8,128)(2,1)S(1)}, u32[]{:S(2)}) copy-start(bf16[1,1,1,3,224,224]{5,4,3,2,1,0:T(8,128)(2,1)S(1)} %collective-permute-done.fa_ref) | copy-start | bytes 903172
  36.4 17.6 %copy-start.7 = (bf16[160,1176]{1,0:T(8,128)(2,1)}, bf16[160,1176]{1,0:T(8,128)(2,1)S(1)}, u32[]{:S(2)}) copy-start(bf16[160,1176]{1,0:T(8,128)(2,1)S(1)} %collective-permute-done.3.refs_2_) | copy-start | bytes 1128964
  36.4 17.3 %copy-start.8 = (bf16[160,1176]{1,0:T(8,128)(2,1)}, bf16[160,1176]{1,0:T(8,128)(2,1)S(1)}, u32[]{:S(2)}) copy-start(bf16[160,1176]{1,0:T(8,128)(2,1)S(1)} %collective-permute-done.2.refs_1_) | copy-start | bytes 1128964
  40.6 5.5 %copy-start.9 = (bf16[160,1176]{1,0:T(8,128)(2,1)}, bf16[160,1176]{1,0:T(8,128)(2,1)S(1)}, u32[]{:S(2)}) copy-start(bf16[160,1176]{1,0:T(8,128)(2,1)S(1)} %collective-permute-done.1.refs_0_) | copy-start | bytes 1128964
  46.1 8.2 %copy-start.11 = (f32[1280]{0:T(1024)S(1)}, f32[1280]{0:T(1024)}, u32[]{:S(2)}) copy-start(f32[1280]{0:T(1024)} %param.12) | copy-start | bytes 15364
  46.1 8.8 %copy-start.12 = (s32[1,1,512]{2,1,0:T(1,128)S(1)}, s32[1,1,512]{2,1,0:T(1,128)}, u32[]{:S(2)}) copy-start(s32[1,1,512]{2,1,0:T(1,128)} %param.13) | copy-start | bytes 6148
  47.3 8.4 %copy-start.4 = (bf16[16,296,128]{2,1,0:T(8,128)(2,1)}, bf16[16,296,128]{2,1,0:T(8,128)(2,1)S(1)}, u32[]{:S(2)}) copy-start(bf16[16,296,128]{2,1,0:T(8,128)(2,1)S(1)} %all-to-all-done.1.arr_ref) | copy-start | bytes 3637252
  47.3 37.4 %all-to-all-start = ((bf16[16,296,128]{2,1,0:T(8,128)(2,1)}), bf16[16,296,128]{2,1,0:T(8,128)(2,1)S(1)}, u32[]{:S(2)}, u32[]{:S(2)}) async-start(bf16[16,296,128]{2,1,0:T(8,128)(2,1)} %patch_rows.3), calls=%async_computation | async-start | bytes 2424832 | tf_op jit(solution)/shard_map/all_to_all | solution.py:400
  53.5 2.8 %collective-permute-start.4 = (bf16[160,1176]{1,0:T(8,128)(2,1)}, bf16[160,1176]{1,0:T(8,128)(2,1)}, u32[]{:S(2)}, u32[]{:S(2)}) collective-permute-start(bf16[160,1176]{1,0:T(8,128)(2,1)} %copy-done.9), channel_id=1, source_target_pairs={{0,16},{16,0},{1,17},{17,1},{2,18},{18,2},{3,19},{19,3},{4,20},{20... | collective-permute-start | bytes 1128968 | tf_op jit(solution)/shard_map/ppermute | solution.py:401
  53.7 2.7 %collective-permute-start.5 = (bf16[160,1176]{1,0:T(8,128)(2,1)S(1)}, bf16[160,1176]{1,0:T(8,128)(2,1)}, u32[]{:S(2)}, u32[]{:S(2)}) collective-permute-start(bf16[160,1176]{1,0:T(8,128)(2,1)S(1)} %collective-permute-done.2.refs_1_), channel_id=1, source_target_pairs={{0,16},{16,0},{1,17},{17,1},{2,18},{18,2},{3,19},{19,3},{4,20},{20... | collective-permute-start | bytes 1128968 | tf_op jit(solution)/shard_map/ppermute | solution.py:401
  54.0 2.5 %collective-permute-start.6 = (bf16[160,1176]{1,0:T(8,128)(2,1)S(1)}, bf16[160,1176]{1,0:T(8,128)(2,1)}, u32[]{:S(2)}, u32[]{:S(2)}) collective-permute-start(bf16[160,1176]{1,0:T(8,128)(2,1)S(1)} %collective-permute-done.3.refs_2_), channel_id=1, source_target_pairs={{0,16},{16,0},{1,17},{17,1},{2,18},{18,2},{3,19},{19,3},{4,20},{20... | collective-permute-start | bytes 1128968 | tf_op jit(solution)/shard_map/ppermute | solution.py:401
  85.8 14.0 %copy-start.3 = (s32[3]{0:T(128)S(1)}, s32[3]{0:T(128)}, u32[]{:S(2)}) copy-start(s32[3]{0:T(128)} %pad_add_fusion.place_ref.core_ref) | copy-start | bytes 40
  95.5 4.3 %collective-permute-start.7 = (bf16[512,1280]{1,0:T(8,128)(2,1)}, bf16[512,1280]{1,0:T(8,128)(2,1)S(1)}, u32[]{:S(2)}, u32[]{:S(2)}) collective-permute-start(bf16[512,1280]{1,0:T(8,128)(2,1)} %get-tuple-element.26.grad0_ref), channel_id=1, source_target_pairs={{0,16},{16,0},{1,17},{17,1},{2,18},{18,2},{3,19},{19,3},{4,20},{20... | collective-permute-start | bytes 3932168 | tf_op jit(solution)/shard_map/ppermute | solution.py:408
  95.6 4.2 %collective-permute-start.8 = (bf16[512,640]{1,0:T(8,128)(2,1)}, bf16[512,640]{1,0:T(8,128)(2,1)S(1)}, u32[]{:S(2)}, u32[]{:S(2)}) collective-permute-start(bf16[512,640]{1,0:T(8,128)(2,1)} %get-tuple-element.28), channel_id=1, source_target_pairs={{0,16},{16,0},{1,17},{17,1},{2,18},{18,2},{3,19},{19,3},{4,20},{20... | collective-permute-start | bytes 1966088 | tf_op jit(solution)/shard_map/ppermute | solution.py:407
  106.2 8.4 %collective-permute-start.9 = (bf16[1600,128]{1,0:T(8,128)(2,1)S(1)}, bf16[1600,128]{1,0:T(8,128)(2,1)S(1)}, u32[]{:S(2)}, u32[]{:S(2)}) collective-permute-start(bf16[1600,128]{1,0:T(8,128)(2,1)S(1)} %get-tuple-element.31), channel_id=1, source_target_pairs={{0,1},{16,20},{1,2},{17,21},{2,3},{18,22},{3,0},{19,23},{4,5},{20,... | collective-permute-start | bytes 1228808 | tf_op jit(solution)/shard_map/ppermute | solution.py:410
  107.5 10.8 %collective-permute-start.10 = (bf16[1600,128]{1,0:T(8,128)(2,1)S(1)}, bf16[1600,128]{1,0:T(8,128)(2,1)S(1)}, u32[]{:S(2)}, u32[]{:S(2)}) collective-permute-start(bf16[1600,128]{1,0:T(8,128)(2,1)S(1)} %get-tuple-element.32), channel_id=1, source_target_pairs={{0,3},{16,28},{1,0},{17,29},{2,1},{18,30},{3,2},{19,31},{4,7},{20,... | collective-permute-start | bytes 1228808 | tf_op jit(solution)/shard_map/ppermute | solution.py:410
  109.0 10.7 %collective-permute-start.11 = (bf16[1600,128]{1,0:T(8,128)(2,1)S(1)}, bf16[1600,128]{1,0:T(8,128)(2,1)S(1)}, u32[]{:S(2)}, u32[]{:S(2)}) collective-permute-start(bf16[1600,128]{1,0:T(8,128)(2,1)S(1)} %get-tuple-element.33), channel_id=1, source_target_pairs={{0,2},{16,24},{1,3},{17,25},{2,0},{18,26},{3,1},{19,27},{4,6},{20,... | collective-permute-start | bytes 1228808 | tf_op jit(solution)/shard_map/ppermute | solution.py:410
  166.3 7.8 %collective-permute-start.12 = (f32[1600,128]{1,0:T(8,128)S(1)}, f32[1600,128]{1,0:T(8,128)S(1)}, u32[]{:S(2)}, u32[]{:S(2)}) collective-permute-start(f32[1600,128]{1,0:T(8,128)S(1)} %bitcast.10), channel_id=1, source_target_pairs={{0,16},{16,0},{1,17},{17,1},{2,18},{18,2},{3,19},{19,3},{4,20},{20... | collective-permute-start | bytes 2457608 | tf_op jit(solution)/shard_map/ppermute | solution.py:421
  (4 other events, 4.3 us)
